TPU v7x, 256 devices: a whole 4x4x8 slice. The times are simulated.
256 devices in a mesh: rep: 32 (over y_lo, z, core), tm: 4 (over x), space: 2 (over y_hi).
Axes of the slice: x: 4, y: 4 (y_hi: 2, y_lo: 2; y = y_hi * 2 + y_lo), z: 8, core: 2. Of those that a mesh axis runs over, the one named last changes fastest.
Arguments:
- spins: float32 [160, 3, 64, 4096], P('rep', None, 'tm', 'space'), may hold values from -4 to 4
- bond_right: float32 [4096], P('space'), may hold values from -4 to 4
- bond_down: float32 [4096], P('space'), may hold values from -4 to 4
- betas: float32 [160], P('rep'), may hold values from 0.2 to 2
- time_coupling: float32 [160], P('rep'), may hold values from 0.1 to 1
- thresholds: int32 [2, 160, 64, 4096], P(None, 'rep', 'tm', 'space'), may hold values from 0 to 8191
- partner: int32 [160], P('rep'), may hold values from 0 to 159, as said below
- accept: int32 [160], P('rep'), may hold values from 0 to 1, as said below
Outputs:
- swapped: float32 [160, 3, 64, 4096], P('rep', None, 'tm', 'space')
- energies: float32 [160, 64], P('rep', 'tm')
Inputs may be any that keep to these rules, and one draw needn't show every extreme that they name: partner[r] is r - 1, r or r + 1, and partner[partner[r]] = r; partner[r] = r + 1 wherever r % 5 = 4 and r + 1 < 160. accept[r] = accept[partner[r]], accept[r] = 0 where partner[r] = r, and accept[r] = 1 wherever r % 5 = 4 and r + 1 < 160.
All inputs are finite; a program needn't handle non-finite values.
Results may differ from a plain program's by a relative error of at most 0.0001.
Values sent between devices are 32-bit elements; how exact they have to be, the bound alone decides.
No kernel may reach another device: no remote copies, remote signals or barrier semaphores. Data moves between devices by JAX's collectives and lax.ppermute only.
A program may use at most 64 MiB of HBM per device.

v0:
```python
import jax
import jax.numpy as jnp
from jax import lax
from jax.sharding import PartitionSpec as P

LY = 64


def shifted(x, axis, by):
    size = lax.axis_size(axis)
    return lax.ppermute(x, axis, [(i, (i + by) % size) for i in range(size)])


def extended_2(cells, sides, width):
    for axis, dim in sides:
        count = lax.axis_size(axis)
        head = lax.slice_in_dim(cells, 0, width, axis=dim)
        tail = lax.slice_in_dim(cells, cells.shape[dim] - width, cells.shape[dim], axis=dim)
        cells = jnp.concatenate(
            [
                lax.ppermute(tail, axis, [(i, (i + 1) % count) for i in range(count)]),
                cells,
                lax.ppermute(head, axis, [((i + 1) % count, i) for i in range(count)]),
            ],
            axis=dim,
        )
    return cells


def copy_for_each(x, axis):
    size = lax.axis_size(axis)
    return lax.all_to_all(jnp.broadcast_to(x[None], (size, *x.shape)), axis, 0, 0, tiled=True)


def of_everyone(x, axis):
    return copy_for_each(x, axis).sum(axis=0)


def from_behind(x, axis, by):
    size = lax.axis_size(axis)
    pairs = [(i, i + by) for i in range(size) if 0 <= i + by < size]
    return lax.ppermute(x, axis, pairs)


def choose(extended, offset):
    return jnp.where(
        offset == -1, extended[:-2], jnp.where(offset == 1, extended[2:], extended[1:-1])
    )


def on_device(spins, bond_right, bond_down, betas, time_coupling, thresholds, partner, accept):
    reps, comps, slices, local = spins.shape
    row_len = LY
    first_row = lax.axis_index("space") * (local // row_len)
    first_slice = lax.axis_index("tm") * slices
    first_rep = lax.axis_index("rep") * reps
    lattice_total = local * lax.axis_size("space")
    flat = jnp.arange(local, dtype=jnp.int32)
    column = flat % row_len
    row = flat // row_len + first_row
    level = jnp.arange(slices, dtype=jnp.int32) + first_slice
    parity = (row[None, :] + column[None, :] + level[:, None]) % 2
    above_bonds = shifted(bond_down[local - row_len :], "space", 1)
    bond_up = jnp.concatenate([above_bonds, bond_down[: local - row_len]], axis=0)
    bond_left = jnp.where(
        column == 0, jnp.roll(bond_right, -(row_len - 1)), jnp.roll(bond_right, 1)
    )
    beta_col = betas[:, None, None, None]
    coupling_col = time_coupling[:, None, None, None]
    state = spins
    field_space = jnp.zeros_like(spins)
    for half in range(2):
        planes = extended_2(state, (("tm", 2),), 1)
        lattice_rows = extended_2(state, (("space", 3),), row_len)
        down = lattice_rows[..., 2 * row_len :]
        upper = lattice_rows[..., :local]
        right = jnp.where(
            column == row_len - 1, jnp.roll(state, row_len - 1, axis=3), jnp.roll(state, -1, axis=3)
        )
        left = jnp.where(
            column == 0, jnp.roll(state, -(row_len - 1), axis=3), jnp.roll(state, 1, axis=3)
        )
        field_space = bond_down * down + bond_up * upper + bond_right * right + bond_left * left
        field = beta_col * field_space + coupling_col * (planes[:, :, 2:] + planes[:, :, :-2])
        weight = (thresholds[half].astype(jnp.float32) + 0.5) / 8192.0
        moved = state + weight[:, None] * field
        fresh = moved / jnp.sqrt(0.25 + jnp.sum(moved * moved, axis=1, keepdims=True))
        state = jnp.where(parity == half, fresh, state)
    site_terms = jnp.where(parity == 1, jnp.sum(state * field_space, axis=1), 0.0)
    partial_energy = -jnp.sum(site_terms, axis=-1) / lattice_total
    offset = jnp.where(accept == 1, partner - (first_rep + jnp.arange(reps, dtype=jnp.int32)), 0)
    energy = of_everyone(partial_energy, "space")
    lower_state, lower_energy = from_behind((state[-1:], energy[-1:]), "rep", 1)
    upper_state, upper_energy = from_behind((state[:1], energy[:1]), "rep", -1)
    state_ext = jnp.concatenate([lower_state, state, upper_state], axis=0)
    energy_ext = jnp.concatenate([lower_energy, energy, upper_energy], axis=0)
    swapped = choose(state_ext, offset[:, None, None, None])
    energies = choose(energy_ext, offset[:, None])
    return (swapped, energies)


def solution(mesh):
    placed = (
        P("rep", None, "tm", "space"),
        P("space"),
        P("space"),
        P("rep"),
        P("rep"),
        P(None, "rep", "tm", "space"),
        P("rep"),
        P("rep"),
    )
    return jax.shard_map(
        on_device,
        mesh=mesh,
        in_specs=placed,
        out_specs=(P("rep", None, "tm", "space"), P("rep", "tm")),
        check_vma=False,
    )
```

profile of v0, /device:TPU:113, one launch (start us, length us, event | category | flops | bytes accessed | tf_op | source)
XLA Modules:
  0.0 110.4 jit_solution(17575689019186240186)
XLA Ops:
  0.6 2.7 %copy.152 = f32[5,3,16,2048]{3,0,2,1:T(8,128)S(1)} copy(f32[5,3,16,2048]{3,2,1,0:T(8,128)} %param.8) | data formatting | bytes 3932160 | tf_op args[0]
  4.2 2.9 %collective-permute-start.2 = (f32[5,3,16,64]{3,0,2,1:T(8,128)}, f32[5,3,16,64]{3,0,2,1:T(8,128)}, u32[]{:S(2)}, u32[]{:S(2)}) collective-permute-start(f32[5,3,16,64]{3,0,2,1:T(8,128)} %get-tuple-element.37), channel_id=1, source_target_pairs={{0,1},{1,0},{2,3},{3,2},{4,5},{5,4},{6,7},{7,6},{8,9},{9,8},{10,11... | collective-permute-start | bytes 184328 | tf_op jit(solution)/shard_map/ppermute | solution.py:21
  7.9 2.5 %collective-permute-start.3 = (f32[5,3,1,2048]{3,0,2,1:T(8,128)}, f32[5,3,1,2048]{3,0,2,1:T(8,128)}, u32[]{:S(2)}, u32[]{:S(2)}) collective-permute-start(f32[5,3,1,2048]{3,0,2,1:T(8,128)} %get-tuple-element.46), channel_id=1, source_target_pairs={{2,0},{4,2},{6,4},{0,6},{3,1},{5,3},{7,5},{1,7},{10,8},{12,10},{14... | collective-permute-start | bytes 368648 | tf_op jit(solution)/shard_map/ppermute | solution.py:23
  10.4 1.3 %slice.171 = f32[64]{0:T(128)} slice(f32[2048]{0:T(1024)} %param.10), slice={[1984:2048]} | slice | bytes 512 | tf_op jit(solution)/shard_map/slice | solution.py:63
  11.7 3.8 %fusion.52 = (f32[5,3,16,1985]{3,0,2,1:T(8,128)}, f32[5,3,16,1985]{3,0,2,1:T(8,128)}) fusion(f32[5,3,16,2048]{3,0,2,1:T(8,128)S(1)} %copy.152), kind=kLoop, calls=%fused_computation.93 | loop fusion | bytes 7622400 | tf_op jit(solution)/shard_map/jit(_roll_static)/slice | solution.py:78
  15.6 3.8 %fusion.53 = (f32[5,3,16,2047]{3,0,2,1:T(8,128)}, f32[5,3,16,2047]{3,0,2,1:T(8,128)}) fusion(f32[5,3,16,2048]{3,0,2,1:T(8,128)S(1)} %copy.152), kind=kLoop, calls=%fused_computation.94 | loop fusion | bytes 7860480 | tf_op jit(solution)/shard_map/jit(_roll_static)/slice | solution.py:78
  22.6 2.5 %multiply_bitcast_fusion = (f32[5,16,2048]{2,1,0:T(8,128)}, f32[5,16,2048]{2,1,0:T(8,128)}) fusion(s32[2,5,16,2048]{3,2,1,0:T(8,128)} %param.13), kind=kLoop, calls=%fused_computation.49 | loop fusion | flops 983040 | bytes 2621440 | tf_op jit(solution)/shard_map/div | solution.py:85
  25.7 1.4 %broadcast_compare_fusion = (pred[5]{0:T(512)(128)(4,1)}, s32[5]{0:T(128)S(1)}) fusion(s32[5]{0:T(128)} %param.14, s32[]{:T(128)S(6)} %mul.56, s32[5]{0:T(128)} %param.15), kind=kLoop, calls=%fused_computation.82 | loop fusion | flops 25 | bytes 69 | tf_op jit(solution)/shard_map/eq | solution.py:47
  27.6 1.4 %fusion.29 = (pred[16,2048]{1,0:T(8,128)(4,1)}, pred[16,2048]{1,0:T(8,128)(4,1)S(1)}) fusion(s32[16]{0:T(128)} %iota_add_fusion, s32[2048]{0:T(1024)S(1)} %fusion.37), kind=kLoop, calls=%fused_computation.58 | loop fusion | flops 458752 | bytes 73792 | tf_op jit(solution)/shard_map/eq | solution.py:88
  29.0 1.4 %maximum_select_fusion.4 = f32[2048]{0:T(1024)S(1)} fusion(f32[63]{0:T(128)} %slice.180, f32[1985]{0:T(1024)} %slice.179, f32[2047]{0:T(1024)S(1)} %bitcast.6, f32[1]{0:T(128)} %slice.181), kind=kLoop, calls=%fused_computation.75 | loop fusion | flops 20480 | bytes 24576 | tf_op jit(solution)/shard_map/jit(_where)/select_n | solution.py:65
  30.4 1.5 %copy.135 = f32[5,16,2048]{2,0,1:T(8,128)S(1)} copy(f32[5,16,2048]{2,1,0:T(8,128)} %get-tuple-element.49) | data formatting | bytes 1310720 | tf_op jit(solution)/shard_map/div | solution.py:85
  31.9 2.5 %copy.154 = f32[5,16,2048]{2,0,1:T(8,128)} copy(f32[5,16,2048]{2,1,0:T(8,128)} %get-tuple-element.48) | data formatting | bytes 1310720 | tf_op jit(solution)/shard_map/div | solution.py:85
  35.2 7.4 %multiply_reduce_fusion.2 = (f32[5,16,2048]{2,0,1:T(8,128)S(1)}, f32[5,3,16,2048]{3,0,2,1:T(8,128)S(1)}) fusion(f32[5,3,16,2048]{3,0,2,1:T(8,128)S(1)} %copy.152, f32[5,3,1,2048]{3,0,2,1:T(8,128)} %collective-permute-done.4, f32[5,3,1,2048]{3,0,2,1:T(8,128)} %collective-permute-done.3, f32[5]{0:T(128)S(1)} %copy-done.11, ...), kind=kLoop, calls=%fused_computation.45 | loop fusion | flops 12124160 | bytes 13512744 | tf_op jit(solution)/shard_map/reduce_sum | solution.py:87
  42.9 1.3 %copy-done.2 = f32[5,3,16,2048]{3,2,1,0:T(8,128)S(1)} copy-done((f32[5,3,16,2048]{3,2,1,0:T(8,128)S(1)}, f32[5,3,16,2048]{3,2,1,0:T(8,128)}, u32[]{:S(2)}) %copy-start.2) | copy-done | bytes 1966104
  44.2 1.5 %divide_select_fusion.1 = f32[5,3,16,2048]{3,0,2,1:T(8,128)S(1)} fusion(f32[5,3,16,2048]{3,0,2,1:T(8,128)S(1)} %get-tuple-element.21, f32[5,16,2048]{2,0,1:T(8,128)S(1)} %add_sqrt_fusion.1, pred[16,2048]{1,0:T(8,128)(4,1)S(1)} %get-tuple-element.51, f32[5,3,16,2048]{3,2,1,0:T(8,128)S(1)} %copy-done.2), kind=kLoop, calls=%fused_computation.44 | loop fusion | flops 983040 | bytes 6586368 | tf_op jit(solution)/shard_map/jit(_where)/select_n | solution.py:88
  46.9 1.2 %fusion.47 = (f32[5,3,16,2047]{3,0,2,1:T(8,128)S(1)}, f32[5,3,16,2047]{3,0,2,1:T(8,128)S(1)}) fusion(f32[5,3,16,2048]{3,0,2,1:T(8,128)S(1)} %divide_select_fusion.1), kind=kLoop, calls=%fused_computation.88 | loop fusion | bytes 7860480 | tf_op jit(solution)/shard_map/jit(_roll_static)/slice | solution.py:78
  48.5 3.0 %collective-permute-start.5 = (f32[5,3,16,64]{3,0,2,1:T(8,128)S(1)}, f32[5,3,16,64]{3,0,2,1:T(8,128)S(1)}, u32[]{:S(2)}, u32[]{:S(2)}) collective-permute-start(f32[5,3,16,64]{3,0,2,1:T(8,128)S(1)} %get-tuple-element.24), channel_id=1, source_target_pairs={{1,0},{0,1},{3,2},{2,3},{5,4},{4,5},{7,6},{6,7},{9,8},{8,9},{11,10... | collective-permute-start | bytes 184328 | tf_op jit(solution)/shard_map/ppermute | solution.py:23
  51.6 2.7 %collective-permute-start.7 = (f32[5,3,1,2048]{3,0,2,1:T(8,128)S(1)}, f32[5,3,1,2048]{3,0,2,1:T(8,128)S(1)}, u32[]{:S(2)}, u32[]{:S(2)}) collective-permute-start(f32[5,3,1,2048]{3,0,2,1:T(8,128)S(1)} %get-tuple-element.34), channel_id=1, source_target_pairs={{2,0},{4,2},{6,4},{0,6},{3,1},{5,3},{7,5},{1,7},{10,8},{12,10},{14... | collective-permute-start | bytes 368648 | tf_op jit(solution)/shard_map/ppermute | solution.py:23
  54.6 5.3 %collective-permute-done.6 = f32[5,3,16,64]{3,0,2,1:T(8,128)S(1)} collective-permute-done((f32[5,3,16,64]{3,0,2,1:T(8,128)S(1)}, f32[5,3,16,64]{3,0,2,1:T(8,128)S(1)}, u32[]{:S(2)}, u32[]{:S(2)}) %collective-permute-start.6) | collective-permute-done | bytes 61472 | tf_op jit(solution)/shard_map/ppermute | solution.py:21
  60.1 7.1 %multiply_reduce_fusion.1 = (f32[5,16,2048]{2,0,1:T(8,128)S(1)}, f32[5,3,16,2048]{3,0,2,1:T(8,128)}) fusion(f32[5,3,16,2048]{3,0,2,1:T(8,128)S(1)} %divide_select_fusion.1, f32[5,3,1,2048]{3,0,2,1:T(8,128)S(1)} %collective-permute-done.8, f32[5,3,1,2048]{3,0,2,1:T(8,128)S(1)} %collective-permute-done.7, f32[5]{0:T(128)} %param.12, f32[5]{0:T(128)} %param.11, ...), kind=kLoop, calls=%fused_computation.43 | loop fusion | flops 12124160 | bytes 13512744 | tf_op jit(solution)/shard_map/reduce_sum | solution.py:87
  67.5 3.7 %multiply_reduce_fusion = (f32[5,16,2048]{2,0,1:T(8,128)S(1)}, f32[5,3,16,2048]{3,0,2,1:T(8,128)S(1)}) fusion(f32[5,3,16,2048]{3,0,2,1:T(8,128)} %get-tuple-element.19, f32[5,3,16,2048]{3,0,2,1:T(8,128)S(1)} %divide_select_fusion.1, f32[5,16,2048]{2,0,1:T(8,128)S(1)} %add_sqrt_fusion, f32[5,3,1,2048]{3,0,2,1:T(8,128)S(1)} %collective-permute-done.8, ...), kind=kLoop, calls=%fused_computation.41 | loop fusion | flops 5734400 | bytes 8142888 | tf_op jit(solution)/shard_map/reduce_sum | solution.py:89
  72.2 6.2 %all-to-all-start = ((f32[2,5,16]{2,1,0:T(8,128)}), f32[2,5,16]{2,1,0:T(8,128)S(1)}, u32[]{:S(2)}, u32[]{:S(2)}) async-start(f32[2,5,16]{2,1,0:T(8,128)} %broadcast_in_dim.93), calls=%async_computation | async-start | bytes 16384 | tf_op jit(solution)/shard_map/all_to_all | solution.py:32
  79.2 8.7 %collective-permute-start.9 = (f32[1,3,16,2048]{3,2,1,0:T(8,128)S(1)}, f32[1,3,16,2048]{3,2,1,0:T(8,128)}, u32[]{:S(2)}, u32[]{:S(2)}) collective-permute-start(f32[1,3,16,2048]{3,2,1,0:T(8,128)S(1)} %copy.155), channel_id=1, source_target_pairs={{0,8},{8,16},{16,24},{24,32},{32,40},{40,48},{48,56},{56,64},{64,7... | collective-permute-start | bytes 1179656 | tf_op jit(solution)/shard_map/ppermute | solution.py:42
  88.8 1.9 %collective-permute-start.10 = (f32[1,3,16,2048]{3,2,1,0:T(8,128)}, f32[1,3,16,2048]{3,2,1,0:T(8,128)}, u32[]{:S(2)}, u32[]{:S(2)}) collective-permute-start(f32[1,3,16,2048]{3,2,1,0:T(8,128)} %copy.157), channel_id=1, source_target_pairs={{8,0},{16,8},{24,16},{32,24},{40,32},{48,40},{56,48},{64,56},{72,6... | collective-permute-start | bytes 1179656 | tf_op jit(solution)/shard_map/ppermute | solution.py:42
  90.7 4.9 %collective-permute-start.11 = (f32[1,16]{1,0:T(1,128)S(1)}, f32[1,16]{1,0:T(1,128)S(1)}, u32[]{:S(2)}, u32[]{:S(2)}) collective-permute-start(f32[1,16]{1,0:T(1,128)S(1)} %get-tuple-element.54), channel_id=1, source_target_pairs={{0,8},{8,16},{16,24},{24,32},{32,40},{40,48},{48,56},{56,64},{64,7... | collective-permute-start | bytes 200 | tf_op jit(solution)/shard_map/ppermute | solution.py:42
  95.6 1.9 %collective-permute-start.12 = (f32[1,16]{1,0:T(1,128)S(1)}, f32[1,16]{1,0:T(1,128)S(1)}, u32[]{:S(2)}, u32[]{:S(2)}) collective-permute-start(f32[1,16]{1,0:T(1,128)S(1)} %get-tuple-element.55), channel_id=1, source_target_pairs={{8,0},{16,8},{24,16},{32,24},{40,32},{48,40},{56,48},{64,56},{72,6... | collective-permute-start | bytes 200 | tf_op jit(solution)/shard_map/ppermute | solution.py:42
  97.5 4.1 %collective-permute-done.12 = f32[1,16]{1,0:T(1,128)S(1)} collective-permute-done((f32[1,16]{1,0:T(1,128)S(1)}, f32[1,16]{1,0:T(1,128)S(1)}, u32[]{:S(2)}, u32[]{:S(2)}) %collective-permute-start.12) | collective-permute-done | bytes 96 | tf_op jit(solution)/shard_map/ppermute | solution.py:42
  101.7 1.3 %select_select_fusion = f32[5,16]{1,0:T(8,128)} fusion(f32[5,16]{1,0:T(8,128)S(1)} %reduce_sum.49, f32[6,16]{1,0:T(8,128)S(1)} %get-tuple-element.53, f32[6,16]{1,0:T(8,128)S(1)} %get-tuple-element.52, pred[5]{0:T(512)(128)(4,1)} %broadcast_compare_fusion.1, pred[5]{0:T(512)(128)(4,1)S(1)} %copy-done.13), kind=kLoop, calls=%fused_computation.78 | loop fusion | flops 160 | bytes 1290 | tf_op jit(solution)/shard_map/jit(_where)/select_n | solution.py:46
  103.0 1.4 %copy.156 = f32[1,3,16,2048]{3,0,2,1:T(1,128)S(1)} copy(f32[1,3,16,2048]{3,2,1,0:T(8,128)} %collective-permute-done.9) | data formatting | bytes 786432 | tf_op jit(solution)/shard_map/ppermute | solution.py:42
  104.4 1.4 %copy.158 = f32[1,3,16,2048]{3,0,2,1:T(1,128)S(1)} copy(f32[1,3,16,2048]{3,2,1,0:T(8,128)} %collective-permute-done.10) | data formatting | bytes 786432 | tf_op jit(solution)/shard_map/ppermute | solution.py:42
  105.9 2.2 %fusion.1 = f32[5,3,16,2048]{3,0,2,1:T(8,128)S(1)} fusion(f32[5,3,16,2048]{3,0,2,1:T(8,128)S(1)} %get-tuple-element.15, f32[1,3,16,2048]{3,0,2,1:T(1,128)S(1)} %copy.158, f32[1,3,16,2048]{3,0,2,1:T(1,128)S(1)} %copy.156, pred[5]{0:T(512)(128)(4,1)} %broadcast_compare_fusion.1, pred[5]{0:T(512)(128)(4,1)S(1)} %copy-done.13), kind=kLoop, calls=%fused_computation.2 | loop fusion | flops 1966080 | bytes 4718602 | tf_op jit(solution)/shard_map/jit(_where)/select_n | solution.py:46
  108.0 2.4 %copy.161 = f32[5,3,16,2048]{3,2,1,0:T(8,128)} copy(f32[5,3,16,2048]{3,0,2,1:T(8,128)S(1)} %fusion.1) | data formatting | bytes 3932160
  (74 shorter events, 12.3 us)
Async XLA Ops:
  4.1 31.0 %collective-permute-start = (f32[5,3,16,64]{3,0,2,1:T(8,128)}, f32[5,3,16,64]{3,0,2,1:T(8,128)}, u32[]{:S(2)}, u32[]{:S(2)}) collective-permute-start(f32[5,3,16,64]{3,0,2,1:T(8,128)} %get-tuple-element.36), channel_id=1, source_target_pairs={{1,0},{0,1},{3,2},{2,3},{5,4},{4,5},{7,6},{6,7},{9,8},{8,9},{11,10... | collective-permute-start | bytes 184328 | tf_op jit(solution)/shard_map/ppermute | solution.py:23
  4.2 31.0 %collective-permute-start.2 = (f32[5,3,16,64]{3,0,2,1:T(8,128)}, f32[5,3,16,64]{3,0,2,1:T(8,128)}, u32[]{:S(2)}, u32[]{:S(2)}) collective-permute-start(f32[5,3,16,64]{3,0,2,1:T(8,128)} %get-tuple-element.37), channel_id=1, source_target_pairs={{0,1},{1,0},{2,3},{3,2},{4,5},{5,4},{6,7},{7,6},{8,9},{9,8},{10,11... | collective-permute-start | bytes 184328 | tf_op jit(solution)/shard_map/ppermute | solution.py:21
  7.9 27.3 %collective-permute-start.3 = (f32[5,3,1,2048]{3,0,2,1:T(8,128)}, f32[5,3,1,2048]{3,0,2,1:T(8,128)}, u32[]{:S(2)}, u32[]{:S(2)}) collective-permute-start(f32[5,3,1,2048]{3,0,2,1:T(8,128)} %get-tuple-element.46), channel_id=1, source_target_pairs={{2,0},{4,2},{6,4},{0,6},{3,1},{5,3},{7,5},{1,7},{10,8},{12,10},{14... | collective-permute-start | bytes 368648 | tf_op jit(solution)/shard_map/ppermute | solution.py:23
  10.4 24.8 %collective-permute-start.4 = (f32[5,3,1,2048]{3,0,2,1:T(8,128)}, f32[5,3,1,2048]{3,0,2,1:T(8,128)}, u32[]{:S(2)}, u32[]{:S(2)}) collective-permute-start(f32[5,3,1,2048]{3,0,2,1:T(8,128)} %get-tuple-element.47), channel_id=1, source_target_pairs={{0,2},{2,4},{4,6},{6,0},{1,3},{3,5},{5,7},{7,1},{8,10},{10,12},{12... | collective-permute-start | bytes 368648 | tf_op jit(solution)/shard_map/ppermute | solution.py:21
  11.7 22.7 %collective-permute-start.1 = (f32[64]{0:T(128)}, f32[64]{0:T(128)}, u32[]{:S(2)}, u32[]{:S(2)}) collective-permute-start(f32[64]{0:T(128)} %slice.171), channel_id=1, source_target_pairs={{0,1},{1,0},{2,3},{3,2},{4,5},{5,4},{6,7},{7,6},{8,9},{9,8},{10,11... | collective-permute-start | bytes 776 | tf_op jit(solution)/shard_map/ppermute | solution.py:11
  15.6 4.7 %copy-start.6 = (f32[2048]{0:T(1024)S(1)}, f32[2048]{0:T(1024)}, u32[]{:S(2)}) copy-start(f32[2048]{0:T(1024)} %param.9) | copy-start | bytes 24580
  25.6 9.5 %copy-start = (f32[5,3,16,1985]{3,0,2,1:T(8,128)S(1)}, f32[5,3,16,1985]{3,0,2,1:T(8,128)}, u32[]{:S(2)}) copy-start(f32[5,3,16,1985]{3,0,2,1:T(8,128)} %get-tuple-element.40) | copy-start | bytes 5716804
  25.6 9.6 %copy-start.3 = (f32[5,3,16,1]{3,0,2,1:T(8,128)S(1)}, f32[5,3,16,1]{3,0,2,1:T(8,128)}, u32[]{:S(2)}) copy-start(f32[5,3,16,1]{3,0,2,1:T(8,128)} %get-tuple-element.44) | copy-start | bytes 2884
  25.6 9.6 %copy-start.4 = (f32[5,3,16,1]{3,0,2,1:T(8,128)S(1)}, f32[5,3,16,1]{3,0,2,1:T(8,128)}, u32[]{:S(2)}) copy-start(f32[5,3,16,1]{3,0,2,1:T(8,128)} %get-tuple-element.45) | copy-start | bytes 2884
  25.6 9.6 %copy-start.9 = (pred[2048]{0:T(1024)(128)(4,1)S(1)}, pred[2048]{0:T(1024)(128)(4,1)}, u32[]{:S(2)}) copy-start(pred[2048]{0:T(1024)(128)(4,1)} %fusion.38) | copy-start | bytes 6148
  25.7 9.6 %copy-start.11 = (f32[5]{0:T(128)S(1)}, f32[5]{0:T(128)}, u32[]{:S(2)}) copy-start(f32[5]{0:T(128)} %param.12) | copy-start | bytes 64
  25.7 9.6 %copy-start.12 = (f32[5]{0:T(128)S(1)}, f32[5]{0:T(128)}, u32[]{:S(2)}) copy-start(f32[5]{0:T(128)} %param.11) | copy-start | bytes 64
  30.4 12.2 %copy-start.10 = (pred[2048]{0:T(1024)(128)(4,1)}, pred[2048]{0:T(1024)(128)(4,1)S(1)}, u32[]{:S(2)}) copy-start(pred[2048]{0:T(1024)(128)(4,1)S(1)} %fusion.39) | copy-start | bytes 6148
  35.2 7.5 %copy-start.8 = (f32[2048]{0:T(1024)}, f32[2048]{0:T(1024)S(1)}, u32[]{:S(2)}) copy-start(f32[2048]{0:T(1024)S(1)} %pad_maximum_fusion.10) | copy-start | bytes 24580
  42.6 1.5 %copy-start.2 = (f32[5,3,16,2048]{3,2,1,0:T(8,128)S(1)}, f32[5,3,16,2048]{3,2,1,0:T(8,128)}, u32[]{:S(2)}) copy-start(f32[5,3,16,2048]{3,2,1,0:T(8,128)} %param.8) | copy-start | bytes 5898244
  48.2 11.9 %copy-start.1 = (f32[5,16,2048]{2,0,1:T(8,128)S(1)}, f32[5,16,2048]{2,0,1:T(8,128)}, u32[]{:S(2)}) copy-start(f32[5,16,2048]{2,0,1:T(8,128)} %copy.154) | copy-start | bytes 1966084
  48.2 11.9 %copy-start.7 = (f32[2048]{0:T(1024)S(1)}, f32[2048]{0:T(1024)}, u32[]{:S(2)}) copy-start(f32[2048]{0:T(1024)} %param.10) | copy-start | bytes 24580
  48.5 6.1 %collective-permute-start.5 = (f32[5,3,16,64]{3,0,2,1:T(8,128)S(1)}, f32[5,3,16,64]{3,0,2,1:T(8,128)S(1)}, u32[]{:S(2)}, u32[]{:S(2)}) collective-permute-start(f32[5,3,16,64]{3,0,2,1:T(8,128)S(1)} %get-tuple-element.24), channel_id=1, source_target_pairs={{1,0},{0,1},{3,2},{2,3},{5,4},{4,5},{7,6},{6,7},{9,8},{8,9},{11,10... | collective-permute-start | bytes 184328 | tf_op jit(solution)/shard_map/ppermute | solution.py:23
  51.5 8.4 %collective-permute-start.6 = (f32[5,3,16,64]{3,0,2,1:T(8,128)S(1)}, f32[5,3,16,64]{3,0,2,1:T(8,128)S(1)}, u32[]{:S(2)}, u32[]{:S(2)}) collective-permute-start(f32[5,3,16,64]{3,0,2,1:T(8,128)S(1)} %get-tuple-element.25), channel_id=1, source_target_pairs={{0,1},{1,0},{2,3},{3,2},{4,5},{5,4},{6,7},{7,6},{8,9},{9,8},{10,11... | collective-permute-start | bytes 184328 | tf_op jit(solution)/shard_map/ppermute | solution.py:21
  51.6 8.3 %collective-permute-start.7 = (f32[5,3,1,2048]{3,0,2,1:T(8,128)S(1)}, f32[5,3,1,2048]{3,0,2,1:T(8,128)S(1)}, u32[]{:S(2)}, u32[]{:S(2)}) collective-permute-start(f32[5,3,1,2048]{3,0,2,1:T(8,128)S(1)} %get-tuple-element.34), channel_id=1, source_target_pairs={{2,0},{4,2},{6,4},{0,6},{3,1},{5,3},{7,5},{1,7},{10,8},{12,10},{14... | collective-permute-start | bytes 368648 | tf_op jit(solution)/shard_map/ppermute | solution.py:23
  54.3 5.9 %collective-permute-start.8 = (f32[5,3,1,2048]{3,0,2,1:T(8,128)S(1)}, f32[5,3,1,2048]{3,0,2,1:T(8,128)S(1)}, u32[]{:S(2)}, u32[]{:S(2)}) collective-permute-start(f32[5,3,1,2048]{3,0,2,1:T(8,128)S(1)} %get-tuple-element.35), channel_id=1, source_target_pairs={{0,2},{2,4},{4,6},{6,0},{1,3},{3,5},{5,7},{7,1},{8,10},{10,12},{12... | collective-permute-start | bytes 368648 | tf_op jit(solution)/shard_map/ppermute | solution.py:21
  67.5 3.7 %copy-start.5 = (pred[16,2048]{1,0:T(8,128)(4,1)S(1)}, pred[16,2048]{1,0:T(8,128)(4,1)}, u32[]{:S(2)}) copy-start(pred[16,2048]{1,0:T(8,128)(4,1)} %get-tuple-element.50) | copy-start | bytes 98308
  71.2 30.4 %copy-start.13 = (pred[5]{0:T(512)(128)(4,1)S(1)}, pred[5]{0:T(512)(128)(4,1)}, u32[]{:S(2)}) copy-start(pred[5]{0:T(512)(128)(4,1)} %get-tuple-element.16) | copy-start | bytes 19
  72.2 18.5 %all-to-all-start = ((f32[2,5,16]{2,1,0:T(8,128)}), f32[2,5,16]{2,1,0:T(8,128)S(1)}, u32[]{:S(2)}, u32[]{:S(2)}) async-start(f32[2,5,16]{2,1,0:T(8,128)} %broadcast_in_dim.93), calls=%async_computation | async-start | bytes 16384 | tf_op jit(solution)/shard_map/all_to_all | solution.py:32
  79.2 23.8 %collective-permute-start.9 = (f32[1,3,16,2048]{3,2,1,0:T(8,128)S(1)}, f32[1,3,16,2048]{3,2,1,0:T(8,128)}, u32[]{:S(2)}, u32[]{:S(2)}) collective-permute-start(f32[1,3,16,2048]{3,2,1,0:T(8,128)S(1)} %copy.155), channel_id=1, source_target_pairs={{0,8},{8,16},{16,24},{24,32},{32,40},{40,48},{48,56},{56,64},{64,7... | collective-permute-start | bytes 1179656 | tf_op jit(solution)/shard_map/ppermute | solution.py:42
  88.8 15.7 %collective-permute-start.10 = (f32[1,3,16,2048]{3,2,1,0:T(8,128)}, f32[1,3,16,2048]{3,2,1,0:T(8,128)}, u32[]{:S(2)}, u32[]{:S(2)}) collective-permute-start(f32[1,3,16,2048]{3,2,1,0:T(8,128)} %copy.157), channel_id=1, source_target_pairs={{8,0},{16,8},{24,16},{32,24},{40,32},{48,40},{56,48},{64,56},{72,6... | collective-permute-start | bytes 1179656 | tf_op jit(solution)/shard_map/ppermute | solution.py:42
  90.7 6.8 %collective-permute-start.11 = (f32[1,16]{1,0:T(1,128)S(1)}, f32[1,16]{1,0:T(1,128)S(1)}, u32[]{:S(2)}, u32[]{:S(2)}) collective-permute-start(f32[1,16]{1,0:T(1,128)S(1)} %get-tuple-element.54), channel_id=1, source_target_pairs={{0,8},{8,16},{16,24},{24,32},{32,40},{40,48},{48,56},{56,64},{64,7... | collective-permute-start | bytes 200 | tf_op jit(solution)/shard_map/ppermute | solution.py:42
  95.6 6.1 %collective-permute-start.12 = (f32[1,16]{1,0:T(1,128)S(1)}, f32[1,16]{1,0:T(1,128)S(1)}, u32[]{:S(2)}, u32[]{:S(2)}) collective-permute-start(f32[1,16]{1,0:T(1,128)S(1)} %get-tuple-element.55), channel_id=1, source_target_pairs={{8,0},{16,8},{24,16},{32,24},{40,32},{48,40},{56,48},{64,56},{72,6... | collective-permute-start | bytes 200 | tf_op jit(solution)/shard_map/ppermute | solution.py:42
where the time goes:
time: 111 us; the launch traced here: 110 us
  starting transfers between devices  34.9 us (31%)
  other arithmetic  33.1 us (30%)
  local copies, waits for them, and re-layouts  31.5 us (28%)
  waiting for transfers between devices  9.91 us (9%)
    ppermute x4, starting transfers between devices, from_behind(): return lax.ppermute(x, axis, pairs)  17.4 us
    reduce_sum x2, other arithmetic, on_device(): jnp.sum(moved * moved, axis=1, keepdims=True)  14.5 us
    ppermute x4, starting transfers between devices, extended_2(): lax.ppermute(head, axis, [((i + 1) % count, i) for i in range(count)])  8.21 us
    unnamed x30, local copies, waits for them, and re-layouts  6.43 us
    all_to_all x1, starting transfers between devices, copy_for_each(): lax.all_to_all(jnp.broadcast_to(x[None], (size, *x.shape)), axis, 0, 0, t...  6.23 us
    slice x4, local copies, waits for them, and re-layouts, on_device(): jnp.roll(state, -1, axis=3)  5.97 us
    ppermute x4, waiting for transfers between devices, extended_2(): lax.ppermute(tail, axis, [(i, (i + 1) % count) for i in range(count)])  5.54 us
    slice x4, local copies, waits for them, and re-layouts, on_device(): jnp.roll(state, row_len - 1, axis=3)  5.3 us
  transfers between devices with their start and end apart: 14, of which 4 were waited for; matrix products, arithmetic and copies ran while one was open for 27% of the time, Pallas kernels for 0%

commit v1 on v0

v1 whole, which is shorter than its diff:
```python
import jax
import jax.numpy as jnp
from jax import lax
from jax.experimental import pallas as pl
from jax.experimental.pallas import tpu as pltpu
from jax.sharding import PartitionSpec as P

TILES = 16
PLANES = 8
CORE = TILES * PLANES
CORE_MSG = CORE + 2
EDGE = 10
ROWQ = 10
MESSAGE_ROWS = 424
CHUNK = 5
F32 = jnp.float32
VMEM_LIMIT = 48 * 1024 * 1024


def lanes():
    return lax.broadcasted_iota(jnp.int32, (8, 128), 1)


def subs():
    return lax.broadcasted_iota(jnp.int32, (8, 128), 0)


def checker():
    lane = lanes()
    return lax.rem(lane // 64 + lax.rem(lane, 64) + subs(), 2) == 0


def checker_row0(rows):
    lane = lax.broadcasted_iota(jnp.int32, (rows, 128), 1)
    return lax.rem(lane // 64 + lax.rem(lane, 64), 2) == 0


def take(x, index, axis):
    return jnp.take_along_axis(x, index, axis=axis, mode="promise_in_bounds")


def pack_config(spins, thr0, thr1, masks, put):
    mask, flip = masks
    for k in range(TILES):
        for comp in range(3):
            a, b = spins(comp, 0, k), take(spins(comp, 1, k), flip, 0)
            put(comp, k, jnp.where(mask, a, b))
            put(3 + comp, k, jnp.where(mask, b, a))
        a, b = thr0(0, k), take(thr0(1, k), flip, 0)
        put(6, k, (jnp.where(mask, a, b).astype(F32) + 0.5) / 8192.0)
        a, b = thr1(0, k), take(thr1(1, k), flip, 0)
        put(7, k, (jnp.where(mask, b, a).astype(F32) + 0.5) / 8192.0)


def config_reader(spin_buf, thr_buf):
    def spins(comp, half, k):
        return spin_buf[comp, half * 8 : half * 8 + 8, k * 128 : k * 128 + 128]

    def thr(which):
        return lambda half, k: thr_buf[which, half * 8 : half * 8 + 8, k * 128 : k * 128 + 128]

    return spins, thr(0), thr(1)


def edge_message(get, out, base):
    low = lanes() < 64
    last = TILES - 1
    for comp in range(3):
        out[base + comp] = get(3 + comp, 0)
        out[base + 3 + comp] = get(3 + comp, last)
        out[base + 6 + comp] = jnp.where(low, get(comp, 0), get(comp, last))
    out[base + 9] = jnp.where(low, get(6, 0), get(6, last))


def fetch(spins_ref, thr_ref, config, spin_buf, thr_buf, sem, base):
    copies = [
        pltpu.make_async_copy(spins_ref.at[config], spin_buf, sem.at[base]),
        pltpu.make_async_copy(thr_ref.at[0, config], thr_buf.at[0], sem.at[base + 1]),
        pltpu.make_async_copy(thr_ref.at[1, config], thr_buf.at[1], sem.at[base + 2]),
    ]
    for copy in copies:
        copy.start()
    return copies


def far_kernel(spins_ref, thr_ref, beta_ref, coup_ref, core_ref, edge_ref, spin_buf, thr_buf, sem):
    config = jnp.where(lax.rem(lax.axis_index("rep"), 2) == 0, 0, 4)
    copies = fetch(spins_ref, thr_ref, config, spin_buf, thr_buf, sem, 0)
    core_ref[CORE] = jnp.full((8, 128), beta_ref[config], F32)
    core_ref[CORE + 1] = jnp.full((8, 128), coup_ref[config], F32)
    masks = (checker(), 7 - subs())
    for copy in copies:
        copy.wait()

    def put(plane, k, value):
        core_ref[k * PLANES + plane] = value

    pack_config(*config_reader(spin_buf, thr_buf), masks, put)
    edge_message(lambda plane, k: core_ref[k * PLANES + plane], edge_ref, 0)


def near_kernel(
    spins_ref, thr_ref, beta_ref, coup_ref, right_ref, down_ref,
    core_ref, edge_ref, inner_ref, inner_edge_ref, rows_ref,
    spin_buf, thr_buf, sem,
):
    near = jnp.where(lax.rem(lax.axis_index("rep"), 2) == 0, 4, 0)
    copies = [
        fetch(spins_ref, thr_ref, config, spin_buf.at[n], thr_buf.at[n], sem, 3 * n)
        for n, config in enumerate((near, 1, 2, 3))
    ]
    core_ref[CORE] = jnp.full((8, 128), beta_ref[near], F32)
    core_ref[CORE + 1] = jnp.full((8, 128), coup_ref[near], F32)
    last = TILES - 1
    bonds = 3 * EDGE
    inner_edge_ref[bonds] = jnp.zeros((8, 128), F32)
    inner_edge_ref[bonds, 0:1] = down_ref[0:1]
    inner_edge_ref[bonds, 1:2] = down_ref[last : last + 1]
    inner_edge_ref[bonds, 2:3] = right_ref[0:1]
    inner_edge_ref[bonds, 3:4] = right_ref[last : last + 1]
    masks = (checker(), 7 - subs())
    for copy in copies[0]:
        copy.wait()

    def put_core(plane, k, value):
        core_ref[k * PLANES + plane] = value

    pack_config(*config_reader(spin_buf.at[0], thr_buf.at[0]), masks, put_core)
    edge_message(lambda plane, k: core_ref[k * PLANES + plane], edge_ref, 0)
    for n in range(3):
        for copy in copies[n + 1]:
            copy.wait()

        def put(plane, k, value):
            inner_ref[n, k * PLANES + plane] = value
            if plane < 7:
                rows_ref[plane * TILES + k, n : n + 1] = value[0:1]
            if 3 <= plane < 6:
                rows_ref[(plane + 4) * TILES + k, n : n + 1] = value[1:2]

        pack_config(*config_reader(spin_buf.at[n + 1], thr_buf.at[n + 1]), masks, put)
        edge_message(lambda plane, k: inner_ref[n, k * PLANES + plane], inner_edge_ref, n * EDGE)


def slices_kernel(
    rows_ref, x_ref, y_ref, inner_edge_ref, x_edge_ref, y_edge_ref, beta_ref, coup_ref,
    up_ref, down_ref, own_ref,
):
    sub = subs()
    even = checker_row0(8)
    low = lanes() < 64
    swap = jnp.bitwise_xor(lanes(), 1)

    def five(mine, x, y):
        return jnp.where(sub == 3, x, jnp.where(sub == 4, y, mine))

    def row(q, k):
        plane, s = (q, 0) if q < 7 else (q - 4, 1)
        at = k * PLANES + plane
        return five(rows_ref[q * TILES + k], x_ref[at, s : s + 1], y_ref[at, s : s + 1])

    for k in range(TILES):
        p0 = [row(c, k) for c in range(3)]
        p1 = [row(3 + c, k) for c in range(3)]
        w0 = row(6, k)
        second = [row(7 + c, k) for c in range(3)]
        for c in range(3):
            own_ref[k * 3 + c] = p1[c]
        swapped_y, swapped_w = take(second[1], swap, 1), take(w0, swap, 1)
        down = [jnp.where(even, p0[c], p1[c]) for c in range(3)]
        down += [jnp.where(even, second[0], swapped_y), jnp.where(even, second[2], swapped_w)]
        up = [jnp.where(even, p1[c], p0[c]) for c in range(3)]
        up += [jnp.where(even, swapped_y, second[0]), jnp.where(even, swapped_w, second[2])]
        for q in range(CHUNK):
            at = (k * CHUNK + q) * 5
            down_ref[at : at + 5] = down[q][0:5]
            up_ref[at : at + 5] = up[q][0:5]
    for c in range(3):
        merged = []
        for ref, base in ((inner_edge_ref, 0), (inner_edge_ref, EDGE), (inner_edge_ref, 2 * EDGE), (x_edge_ref, 0), (y_edge_ref, 0)):
            merged.append(jnp.where(low[0:1], ref[base + c, 0:1], ref[base + 3 + c, 0:1]))
        corner = five(
            jnp.where(sub == 0, merged[0], jnp.where(sub == 1, merged[1], merged[2])), merged[3], merged[4]
        )
        at = (TILES * CHUNK + c) * 5
        down_ref[at : at + 5] = corner[0:5]
        up_ref[at : at + 5] = corner[0:5]
    at = (TILES * CHUNK + 3) * 5
    down_ref[at:MESSAGE_ROWS] = jnp.zeros((MESSAGE_ROWS - at, 128), F32)
    up_ref[at:MESSAGE_ROWS] = jnp.zeros((MESSAGE_ROWS - at, 128), F32)
    for base, ref in ((0, beta_ref), (1, coup_ref)):
        mine = jnp.where(sub == 0, ref[1], jnp.where(sub == 1, ref[2], ref[3]))
        own_ref[3 * TILES + base] = five(mine, x_ref[CORE + base], y_ref[CORE + base])


def row_neighbours():
    lane = lanes()
    column = lax.rem(lane, 64)
    right = jnp.where(column == 63, lane - 63, lane + 1)
    left = jnp.where(column == 0, lane + 63, lane - 1)
    return right, left


def normalized(moved):
    scale = lax.rsqrt(0.25 + (moved[0] * moved[0] + moved[1] * moved[1] + moved[2] * moved[2]))
    return [m * scale for m in moved]


def sweep_kernel(
    inner_ref, x_ref, y_ref, inner_edge_ref, x_edge_ref, y_edge_ref, own_ref, up_ref, down_ref,
    right_ref, bdown_ref, partner_ref, accept_ref,
    out_ref, energy_ref,
    packed, halo, halo_second, bonds, sem, out_sem, out_buf,
):
    rep = lax.axis_index("rep")
    is_even = lax.rem(rep, 2) == 0
    last = TILES - 1
    sources = [inner_ref.at[0], inner_ref.at[1], inner_ref.at[2], x_ref.at[0:CORE], y_ref.at[0:CORE]]
    copies = [
        pltpu.make_async_copy(source, packed.at[n, PLANES : PLANES + CORE], sem.at[n])
        for n, source in enumerate(sources)
    ]
    for copy in copies:
        copy.start()

    low = lanes() < 64
    sub = subs()
    mask = checker()
    right_at, left_at = row_neighbours()
    flip = 7 - sub

    edge_bonds = 3 * EDGE

    def bond_rows(k):
        if k == -1:
            return inner_edge_ref[edge_bonds, 1:2], inner_edge_ref[edge_bonds, 3:4]
        if k == TILES:
            return inner_edge_ref[edge_bonds, 0:1], inner_edge_ref[edge_bonds, 2:3]
        return bdown_ref[k : k + 1], right_ref[k : k + 1]

    before = jnp.zeros((8, 128), F32)
    for k in range(-1, TILES + 1):
        down, right = (jnp.broadcast_to(row, (8, 128)) for row in bond_rows(k))
        turned = pltpu.roll(down, 64, 1)
        bonds[(k + 1) * 4] = down
        bonds[(k + 1) * 4 + 1] = jnp.where(low, before, turned)
        bonds[(k + 1) * 4 + 2] = right
        bonds[(k + 1) * 4 + 3] = take(right, left_at, 1)
        before = turned

    def space_field(at, above, here, below):
        turned = pltpu.roll(here, 64, 1)
        down = jnp.where(low, turned, below)
        upper = jnp.where(low, above, turned)
        return (
            bonds[at * 4] * down
            + bonds[at * 4 + 1] * upper
            + bonds[at * 4 + 2] * take(here, right_at, 1)
            + bonds[at * 4 + 3] * take(here, left_at, 1)
        )

    even8 = checker_row0(8)
    swap = jnp.bitwise_xor(lanes(), 1)

    def chunk(ref, i):
        at = i * 5
        return ref[at : at + 8]

    beta_rows = own_ref[3 * TILES]
    coup_rows = own_ref[3 * TILES + 1]
    for k in range(TILES):
        for c in range(3):
            up, down = chunk(up_ref, k * CHUNK + c), chunk(down_ref, k * CHUNK + c)
            halo[(k + 1) * 6 + c] = jnp.where(even8, down, up)
            halo[(k + 1) * 6 + 3 + c] = jnp.where(even8, up, down)
    for c in range(3):
        corner = jnp.where(even8, chunk(up_ref, TILES * CHUNK + c), chunk(down_ref, TILES * CHUNK + c))
        halo[3 + c] = corner
        halo[(TILES + 1) * 6 + 3 + c] = corner
    for k in range(TILES):
        a_up, a_down = chunk(up_ref, k * CHUNK + 3), chunk(down_ref, k * CHUNK + 3)
        b_up, b_down = chunk(up_ref, k * CHUNK + 4), chunk(down_ref, k * CHUNK + 4)
        second = [
            jnp.where(even8, a_down, a_up),
            take(jnp.where(even8, a_up, a_down), swap, 1),
            jnp.where(even8, b_down, b_up),
        ]
        weight = take(jnp.where(even8, b_up, b_down), swap, 1)
        moved = []
        for c in range(3):
            above = pltpu.roll(halo[k * 6 + 3 + c], 64, 1)
            below = pltpu.roll(halo[(k + 2) * 6 + 3 + c], 64, 1)
            field = beta_rows * space_field(k + 1, above, halo[(k + 1) * 6 + 3 + c], below)
            field = field + coup_rows * (own_ref[k * 3 + c] + second[c])
            moved.append(halo[(k + 1) * 6 + c] + weight * field)
        fresh = normalized(moved)
        for c in range(3):
            halo_second[k * 3 + c] = fresh[c]

    betas = [own_ref[3 * TILES, n : n + 1] for n in range(5)]
    coups = [own_ref[3 * TILES + 1, n : n + 1] for n in range(5)]
    edges = ((inner_edge_ref, 0), (inner_edge_ref, EDGE), (inner_edge_ref, 2 * EDGE), (x_edge_ref, 0), (y_edge_ref, 0))
    lane = lanes()
    energy_ref[...] = jnp.zeros((8, 128), F32)

    def time_sum(here, outer):
        before = jnp.where(sub == 0, outer, pltpu.roll(here, 1, 0))
        after = jnp.where(sub == 7, here, pltpu.roll(here, 7, 0))
        return before + after

    writes = []
    for n in range(5):
        copies[n].wait()
        ref, base = edges[n]
        work = packed.at[n]
        for c in range(3):
            work[c] = ref[base + 6 + c]
            work[(TILES + 1) * PLANES + c] = ref[base + 6 + c]
            work[3 + c] = ref[base + 3 + c]
            work[(TILES + 1) * PLANES + 3 + c] = ref[base + c]
        work[6] = ref[base + 9]
        work[(TILES + 1) * PLANES + 6] = ref[base + 9]
        beta = jnp.broadcast_to(betas[n], (8, 128))
        coup = jnp.broadcast_to(coups[n], (8, 128))

        def update(p, at, above_at, below_at, outer):
            mine, other = (0, 3) if p == 0 else (3, 0)
            weight = work[at * PLANES + 6 + p]
            fields, moved = [], []
            for c in range(3):
                here = work[at * PLANES + other + c]
                above = pltpu.roll(work[above_at * PLANES + other + c], 64, 1)
                below = pltpu.roll(work[below_at * PLANES + other + c], 64, 1)
                space = space_field(at, above, here, below)
                field = beta * space + coup * time_sum(here, outer(c))
                moved.append(work[at * PLANES + mine + c] + weight * field)
                fields.append(space)
            fresh = normalized(moved)
            for c in range(3):
                work[at * PLANES + mine + c] = fresh[c]
            return fields, fresh

        for at in range(TILES + 2):
            update(
                0, at, max(at - 1, 0), min(at + 1, TILES + 1),
                lambda c: halo[at * 6 + 3 + c, n : n + 1],
            )
        total = jnp.zeros((8, 128), F32)
        for k in range(TILES):
            at = k + 1
            fields, fresh = update(1, at, at - 1, at + 1, lambda c: halo_second[k * 3 + c, n : n + 1])
            total = total + (fresh[0] * fields[0] + fresh[1] * fields[1] + fresh[2] * fields[2])
            for c in range(3):
                p0 = work[at * PLANES + c]
                out_buf[n, c, 0:8, k * 128 : k * 128 + 128] = jnp.where(mask, p0, fresh[c])
                out_buf[n, c, 8:16, k * 128 : k * 128 + 128] = take(jnp.where(mask, fresh[c], p0), flip, 0)
        if n < 3:
            slot = n + 1
        elif n == 3:
            slot = jnp.where(is_even, 4, 0)
        else:
            slot = jnp.where(is_even, 0, 4)
        target = jnp.where(accept_ref[slot] == 1, jnp.clip(partner_ref[slot] - 5 * rep, 0, 4), slot)
        write = pltpu.make_async_copy(out_buf.at[n], out_ref.at[target], out_sem.at[n])
        write.start()
        writes.append(write)
        first = jnp.sum(jnp.where(mask, 0.0, total), axis=1, keepdims=True)
        back = jnp.sum(jnp.where(mask, total, 0.0), axis=1, keepdims=True)
        line = jnp.where(lane == sub, first, 0.0) + jnp.where(lane == 15 - sub, back, 0.0)
        line = jnp.sum(line, axis=0, keepdims=True)
        energy_ref[...] = jnp.where(sub == target, -line / 4096.0, energy_ref[...])
    for write in writes:
        write.wait()


def params():
    return pltpu.CompilerParams(vmem_limit_bytes=VMEM_LIMIT)


def vmem():
    return pl.BlockSpec(memory_space=pltpu.VMEM)


def smem():
    return pl.BlockSpec(memory_space=pltpu.SMEM)


def hbm():
    return pl.BlockSpec(memory_space=pl.ANY)


def shape(*dims):
    return jax.ShapeDtypeStruct(dims, F32)


def on_device(spins, bond_right, bond_down, betas, time_coupling, thresholds, partner, accept):
    ranks, depth = lax.axis_size("rep"), lax.axis_size("tm")
    axes = ("rep", "tm", "space")
    right, down = bond_right.reshape(TILES, 128), bond_down.reshape(TILES, 128)

    def far_of(r):
        other = r - 1 if r % 2 == 0 else r + 1
        return other if 0 <= other < ranks else r

    def near_of(r):
        return r + 1 if r % 2 == 0 else r - 1

    def crosswise(x, of):
        pairs = [
            ((r * depth + t) * 2 + s, (of(r) * depth + t) * 2 + 1 - s)
            for r in range(ranks) for t in range(depth) for s in range(2)
        ]
        return lax.ppermute(x, axes, pairs)

    far_core, far_edge = pl.pallas_call(
        far_kernel,
        out_shape=(shape(CORE_MSG, 8, 128), shape(EDGE, 8, 128)),
        in_specs=[hbm(), hbm(), smem(), smem()],
        out_specs=(vmem(), vmem()),
        scratch_shapes=[
            pltpu.VMEM((3, 16, 2048), F32),
            pltpu.VMEM((2, 16, 2048), jnp.int32),
            pltpu.SemaphoreType.DMA((3,)),
        ],
        compiler_params=params(),
        name="pack_far",
    )(spins, thresholds, betas, time_coupling)
    far_core = lax.ppermute(far_core, "rep", [(r, far_of(r)) for r in range(ranks)])
    far_edge = crosswise(far_edge, far_of)

    near_core, near_edge, inner, inner_edge, rows = pl.pallas_call(
        near_kernel,
        out_shape=(
            shape(CORE_MSG, 8, 128), shape(EDGE, 8, 128), shape(3, CORE, 8, 128),
            shape(3 * EDGE + 1, 8, 128), shape(ROWQ * TILES, 8, 128),
        ),
        in_specs=[hbm(), hbm(), smem(), smem(), vmem(), vmem()],
        out_specs=(vmem(),) * 5,
        scratch_shapes=[
            pltpu.VMEM((4, 3, 16, 2048), F32),
            pltpu.VMEM((4, 2, 16, 2048), jnp.int32),
            pltpu.SemaphoreType.DMA((12,)),
        ],
        compiler_params=params(),
        name="pack_near",
    )(spins, thresholds, betas, time_coupling, right, down)
    near_core = lax.ppermute(near_core, "rep", [(r, near_of(r)) for r in range(ranks)])
    near_edge = crosswise(near_edge, near_of)
    inner_edge = lax.ppermute(inner_edge, "space", [(0, 1), (1, 0)])

    message = shape(MESSAGE_ROWS, 128)
    up, down_msg, own = pl.pallas_call(
        slices_kernel,
        out_shape=(message, message, shape(3 * TILES + 2, 8, 128)),
        in_specs=[vmem()] * 6 + [smem()] * 2,
        out_specs=(vmem(),) * 3,
        compiler_params=params(),
        name="slices",
    )(rows, near_core, far_core, inner_edge, near_edge, far_edge, betas, time_coupling)
    from_before = lax.ppermute(up, "tm", [(t, (t + 1) % depth) for t in range(depth)])
    from_after = lax.ppermute(down_msg, "tm", [((t + 1) % depth, t) for t in range(depth)])

    swapped, energy = pl.pallas_call(
        sweep_kernel,
        out_shape=(shape(5, 3, 16, 2048), shape(8, 128)),
        in_specs=[hbm()] * 3 + [vmem()] * 8 + [smem()] * 2,
        out_specs=(hbm(), vmem()),
        scratch_shapes=[
            pltpu.VMEM((5, (TILES + 2) * PLANES, 8, 128), F32),
            pltpu.VMEM(((TILES + 2) * 6, 8, 128), F32),
            pltpu.VMEM((TILES * 3, 8, 128), F32),
            pltpu.VMEM(((TILES + 2) * 4, 8, 128), F32),
            pltpu.SemaphoreType.DMA((5,)),
            pltpu.SemaphoreType.DMA((5,)),
            pltpu.VMEM((5, 3, 16, 2048), F32),
        ],
        compiler_params=params(),
        name="sweep",
    )(
        inner, near_core, far_core, inner_edge, near_edge, far_edge, own, from_before, from_after,
        right, down, partner, accept,
    )
    energy = energy + lax.ppermute(energy, "space", [(0, 1), (1, 0)])
    return swapped, energy[:5, :16]


def solution(mesh):
    placed = (
        P("rep", None, "tm", "space"),
        P("space"),
        P("space"),
        P("rep"),
        P("rep"),
        P(None, "rep", "tm", "space"),
        P("rep"),
        P("rep"),
    )
    return jax.shard_map(
        on_device,
        mesh=mesh,
        in_specs=placed,
        out_specs=(P("rep", None, "tm", "space"), P("rep", "tm")),
        check_vma=False,
    )
```

time: 111 us -> 49.1 us (0.44)
  the two profiles are of different devices: /device:TPU:113 before, /device:TPU:6 now
where the time goes in v1:
time: 49.1 us; the launch traced here: 48.9 us
  waiting for transfers between devices  17.7 us (36%)
  starting transfers between devices  14.4 us (29%)
  Pallas kernels  11.2 us (23%)
  local copies, waits for them, and re-layouts  4.19 us (9%)
  between operations  0.74 us (2%)
  other arithmetic  0.6 us (1%)
    pallas_call x1, Pallas kernels, on_device(): pl.pallas_call(sweep_kernel, out_shape=(shape(5, 3, 16, 2048), shape(8, 1...  6.52 us
    ppermute x2, waiting for transfers between devices, crosswise(): return lax.ppermute(x, axes, pairs)  6.08 us
    ppermute x1, waiting for transfers between devices, on_device(): lax.ppermute(up, 'tm', [(t, (t + 1) % depth) for t in range(depth)])  5.47 us
    ppermute x1, waiting for transfers between devices, on_device(): energy = energy + lax.ppermute(energy, 'space', [(0, 1), (1, 0)])  4.78 us
    ppermute x2, starting transfers between devices, crosswise(): return lax.ppermute(x, axes, pairs)  4.6 us
    unnamed x18, local copies, waits for them, and re-layouts  4.19 us
    ppermute x1, starting transfers between devices, on_device(): lax.ppermute(near_core, 'rep', [(r, near_of(r)) for r in range(ranks)])  3.33 us
    ppermute x1, starting transfers between devices, on_device(): inner_edge = lax.ppermute(inner_edge, 'space', [(0, 1), (1, 0)])  3.19 us
  transfers between devices with their start and end apart: 8, of which 4 were waited for; matrix products, arithmetic and copies ran while one was open for 0% of the time, Pallas kernels for 6%

profile of v1, /device:TPU:6, one launch (start us, length us, event | category | flops | bytes accessed | tf_op | source)
XLA Modules:
  0.0 48.9 jit_solution(3995061317707588252)
XLA Ops:
  0.6 0.0 copy-start
  0.6 1.5 %copy-done = f32[5,3,16,2048]{3,2,1,0:T(8,128)S(1)} copy-done((f32[5,3,16,2048]{3,2,1,0:T(8,128)S(1)}, f32[5,3,16,2048]{3,2,1,0:T(8,128)}, u32[]{:S(2)}) %copy-start) | copy-done | bytes 1966104
  2.2 1.3 %copy-done.1 = s32[2,5,16,2048]{3,2,1,0:T(8,128)S(1)} copy-done((s32[2,5,16,2048]{3,2,1,0:T(8,128)S(1)}, s32[2,5,16,2048]{3,2,1,0:T(8,128)}, u32[]{:S(2)}) %copy-start.1) | copy-done | bytes 1310744
  3.5 0.7 %copy-done.5 = f32[5]{0:T(128)S(1)} copy-done((f32[5]{0:T(128)S(1)}, f32[5]{0:T(128)}, u32[]{:S(2)}) %copy-start.5) | copy-done | bytes 44
  4.2 0.7 %copy-done.6 = f32[5]{0:T(128)S(1)} copy-done((f32[5]{0:T(128)S(1)}, f32[5]{0:T(128)}, u32[]{:S(2)}) %copy-start.6) | copy-done | bytes 44
  4.8 1.2 %pack_far.1 = (f32[130,8,128]{2,1,0:T(8,128)S(1)}, f32[10,8,128]{2,1,0:T(8,128)S(1)}) custom-call(f32[5,3,16,2048]{3,2,1,0:T(8,128)S(1)} %copy-done, s32[2,5,16,2048]{3,2,1,0:T(8,128)S(1)} %copy-done.1, f32[5]{0:T(128)S(1)} %copy-done.5, f32[5]{0:T(128)S(1)} %copy-done.6), custom_call_target="tpu_custom_call" | custom-call | tf_op jit(solution)/shard_map/pack_far/pallas_call | solution.py:415
  6.0 0.7 %collective-permute-start.1 = (f32[130,8,128]{2,1,0:T(8,128)S(1)}, f32[130,8,128]{2,1,0:T(8,128)S(1)}, u32[]{:S(2)}, u32[]{:S(2)}) collective-permute-start(f32[130,8,128]{2,1,0:T(8,128)S(1)} %get-tuple-element.16), channel_id=1, source_target_pairs={{0,0},{8,16},{16,8},{24,32},{32,24},{40,48},{48,40},{56,64},{64,56... | collective-permute-start | bytes 1597448 | tf_op jit(solution)/shard_map/ppermute | solution.py:428
  6.7 0.0 copy-done.2
  6.7 0.0 copy-done.3
  6.7 0.0 copy-done.4
  6.7 0.0 copy-start.7
  6.7 0.0 copy-start.8
  6.8 2.8 %pack_near.1 = (f32[130,8,128]{2,1,0:T(8,128)S(1)}, f32[10,8,128]{2,1,0:T(8,128)S(1)}, f32[3,128,8,128]{3,2,1,0:T(8,128)S(1)}, f32[31,8,128]{2,1,0:T(8,128)S(1)}, f32[160,8,128]{2,1,0:T(8,128)S(1)}) custom-call(f32[5,3,16,2048]{3,2,1,0:T(8,128)} %spins_ref.3, s32[2,5,16,2048]{3,2,1,0:T(8,128)S(1)} %copy-done.2, f32[5]{0:T(128)S(1)} %copy-done.5, ...), custom_call_target="tpu_custom_call" | custom-call | tf_op jit(solution)/shard_map/pack_near/pallas_call | solution.py:431
  9.6 3.3 %collective-permute-start = (f32[130,8,128]{2,1,0:T(8,128)S(1)}, f32[130,8,128]{2,1,0:T(8,128)S(1)}, u32[]{:S(2)}, u32[]{:S(2)}) collective-permute-start(f32[130,8,128]{2,1,0:T(8,128)S(1)} %get-tuple-element.15), channel_id=1, source_target_pairs={{0,8},{8,0},{16,24},{24,16},{32,40},{40,32},{48,56},{56,48},{64,72... | collective-permute-start | bytes 1597448 | tf_op jit(solution)/shard_map/ppermute | solution.py:447
  12.9 3.2 %collective-permute-start.2 = (f32[31,8,128]{2,1,0:T(8,128)S(1)}, f32[31,8,128]{2,1,0:T(8,128)S(1)}, u32[]{:S(2)}, u32[]{:S(2)}) collective-permute-start(f32[31,8,128]{2,1,0:T(8,128)S(1)} %get-tuple-element.17), channel_id=1, source_target_pairs={{0,1},{1,0},{2,3},{3,2},{4,5},{5,4},{6,7},{7,6},{8,9},{9,8},{10,11... | collective-permute-start | bytes 380936 | tf_op jit(solution)/shard_map/ppermute | solution.py:449
  16.1 0.3 collective-permute-start.4
  16.5 4.3 %collective-permute-start.3 = (f32[10,8,128]{2,1,0:T(8,128)S(1)}, f32[10,8,128]{2,1,0:T(8,128)S(1)}, u32[]{:S(2)}, u32[]{:S(2)}) collective-permute-start(f32[10,8,128]{2,1,0:T(8,128)S(1)} %get-tuple-element.18), channel_id=1, source_target_pairs={{0,9},{1,8},{2,11},{3,10},{4,13},{5,12},{6,15},{7,14},{8,1},{9,0},... | collective-permute-start | bytes 122888 | tf_op jit(solution)/shard_map/ppermute | solution.py:413
  20.7 6.1 %collective-permute-done.4.y_edge_ref = f32[10,8,128]{2,1,0:T(8,128)S(1)} collective-permute-done((f32[10,8,128]{2,1,0:T(8,128)S(1)}, f32[10,8,128]{2,1,0:T(8,128)S(1)}, u32[]{:S(2)}, u32[]{:S(2)}) %collective-permute-start.4) | collective-permute-done | bytes 40992 | tf_op jit(solution)/shard_map/ppermute | solution.py:413
  26.8 0.0 collective-permute-done.3.x_edge_ref
  26.8 0.0 collective-permute-done.2.inner_edge_ref
  26.8 0.0 collective-permute-done.1.y_ref
  26.8 0.0 collective-permute-done.x_ref
  26.8 0.7 %slices.1 = (f32[424,128]{1,0:T(8,128)S(1)}, f32[424,128]{1,0:T(8,128)S(1)}, f32[50,8,128]{2,1,0:T(8,128)S(1)}) custom-call(f32[160,8,128]{2,1,0:T(8,128)S(1)} %get-tuple-element.20.rows_ref, f32[130,8,128]{2,1,0:T(8,128)S(1)} %collective-permute-done.x_ref, f32[130,8,128]{2,1,0:T(8,128)S(1)} %collective-permute-done.1.y_ref, ...), custom_call_target="tpu_custom_call" | custom-call | tf_op jit(solution)/shard_map/slices/pallas_call | solution.py:452
  27.6 0.6 %collective-permute-start.5 = (f32[424,128]{1,0:T(8,128)S(1)}, f32[424,128]{1,0:T(8,128)S(1)}, u32[]{:S(2)}, u32[]{:S(2)}) collective-permute-start(f32[424,128]{1,0:T(8,128)S(1)} %get-tuple-element.22), channel_id=1, source_target_pairs={{0,2},{2,4},{4,6},{6,0},{1,3},{3,5},{5,7},{7,1},{8,10},{10,12},{12... | collective-permute-start | bytes 651272 | tf_op jit(solution)/shard_map/ppermute | solution.py:460
  28.1 1.5 %collective-permute-start.6 = (f32[424,128]{1,0:T(8,128)S(1)}, f32[424,128]{1,0:T(8,128)S(1)}, u32[]{:S(2)}, u32[]{:S(2)}) collective-permute-start(f32[424,128]{1,0:T(8,128)S(1)} %get-tuple-element.23), channel_id=1, source_target_pairs={{2,0},{4,2},{6,4},{0,6},{3,1},{5,3},{7,5},{1,7},{10,8},{12,10},{14... | collective-permute-start | bytes 651272 | tf_op jit(solution)/shard_map/ppermute | solution.py:461
  29.7 5.5 %collective-permute-done.5.up_ref = f32[424,128]{1,0:T(8,128)S(1)} collective-permute-done((f32[424,128]{1,0:T(8,128)S(1)}, f32[424,128]{1,0:T(8,128)S(1)}, u32[]{:S(2)}, u32[]{:S(2)}) %collective-permute-start.5) | collective-permute-done | bytes 217120 | tf_op jit(solution)/shard_map/ppermute | solution.py:460
  35.1 1.4 %collective-permute-done.6.down_ref = f32[424,128]{1,0:T(8,128)S(1)} collective-permute-done((f32[424,128]{1,0:T(8,128)S(1)}, f32[424,128]{1,0:T(8,128)S(1)}, u32[]{:S(2)}, u32[]{:S(2)}) %collective-permute-start.6) | collective-permute-done | bytes 217120 | tf_op jit(solution)/shard_map/ppermute | solution.py:461
  36.5 0.0 copy-done.8
  36.5 6.5 %sweep.1 = (f32[5,3,16,2048]{3,2,1,0:T(8,128)}, f32[8,128]{1,0:T(8,128)S(1)}) custom-call(f32[3,128,8,128]{3,2,1,0:T(8,128)S(1)} %get-tuple-element.14.inner_ref, f32[130,8,128]{2,1,0:T(8,128)S(1)} %collective-permute-done.x_ref, f32[130,8,128]{2,1,0:T(8,128)S(1)} %collective-permute-done.1.y_ref, f32[31,8,128]{2,1,0:T(8,128)S(1)} %collective-permute-done.2.inner_edge_ref, ...), custom_call_target="tpu_custom_call" | custom-call | tf_op jit(solution)/shard_map/sweep/pallas_call | solution.py:463
  43.1 0.4 collective-permute-start.7
  43.5 4.8 %collective-permute-done.7 = f32[8,128]{1,0:T(8,128)S(1)} collective-permute-done((f32[8,128]{1,0:T(8,128)S(1)}, f32[8,128]{1,0:T(8,128)S(1)}, u32[]{:S(2)}, u32[]{:S(2)}) %collective-permute-start.7) | collective-permute-done | bytes 4128 | tf_op jit(solution)/shard_map/ppermute | solution.py:483
  48.3 0.6 %add.3 = f32[8,128]{1,0:T(8,128)} add(f32[8,128]{1,0:T(8,128)S(1)} %get-tuple-element.25, f32[8,128]{1,0:T(8,128)S(1)} %collective-permute-done.7) | non-fusion elementwise | flops 1024 | bytes 12288 | tf_op jit(solution)/shard_map/add | solution.py:483
  (7 shorter events, 0.0 us)
Async XLA Ops:
  0.6 1.5 %copy-start = (f32[5,3,16,2048]{3,2,1,0:T(8,128)S(1)}, f32[5,3,16,2048]{3,2,1,0:T(8,128)}, u32[]{:S(2)}) copy-start(f32[5,3,16,2048]{3,2,1,0:T(8,128)} %spins_ref.3) | copy-start | bytes 5898244
  2.2 1.3 %copy-start.1 = (s32[2,5,16,2048]{3,2,1,0:T(8,128)S(1)}, s32[2,5,16,2048]{3,2,1,0:T(8,128)}, u32[]{:S(2)}) copy-start(s32[2,5,16,2048]{3,2,1,0:T(8,128)} %thr_ref.3) | copy-start | bytes 3932164
  3.5 0.7 %copy-start.5 = (f32[5]{0:T(128)S(1)}, f32[5]{0:T(128)}, u32[]{:S(2)}) copy-start(f32[5]{0:T(128)} %beta_ref.5) | copy-start | bytes 64
  4.2 0.7 %copy-start.6 = (f32[5]{0:T(128)S(1)}, f32[5]{0:T(128)}, u32[]{:S(2)}) copy-start(f32[5]{0:T(128)} %coup_ref.5) | copy-start | bytes 64
  4.8 1.9 %copy-start.2 = (s32[2,5,16,2048]{3,2,1,0:T(8,128)S(1)}, s32[2,5,16,2048]{3,2,1,0:T(8,128)}, u32[]{:S(2)}) copy-start(s32[2,5,16,2048]{3,2,1,0:T(8,128)} %thr_ref.3) | copy-start | bytes 3932164
  4.8 1.9 %copy-start.3 = (f32[2048]{0:T(1024)S(1)}, f32[2048]{0:T(1024)}, u32[]{:S(2)}) copy-start(f32[2048]{0:T(1024)} %param.9) | copy-start | bytes 24580
  4.8 1.9 %copy-start.4 = (f32[2048]{0:T(1024)S(1)}, f32[2048]{0:T(1024)}, u32[]{:S(2)}) copy-start(f32[2048]{0:T(1024)} %param.10) | copy-start | bytes 24580
  6.0 20.8 %collective-permute-start.1 = (f32[130,8,128]{2,1,0:T(8,128)S(1)}, f32[130,8,128]{2,1,0:T(8,128)S(1)}, u32[]{:S(2)}, u32[]{:S(2)}) collective-permute-start(f32[130,8,128]{2,1,0:T(8,128)S(1)} %get-tuple-element.16), channel_id=1, source_target_pairs={{0,0},{8,16},{16,8},{24,32},{32,24},{40,48},{48,40},{56,64},{64,56... | collective-permute-start | bytes 1597448 | tf_op jit(solution)/shard_map/ppermute | solution.py:428
  6.7 29.8 %copy-start.7 = (s32[5]{0:T(128)S(1)}, s32[5]{0:T(128)}, u32[]{:S(2)}) copy-start(s32[5]{0:T(128)} %partner_ref.1) | copy-start | bytes 64
  6.7 29.8 %copy-start.8 = (s32[5]{0:T(128)S(1)}, s32[5]{0:T(128)}, u32[]{:S(2)}) copy-start(s32[5]{0:T(128)} %accept_ref.1) | copy-start | bytes 64
  9.6 17.2 %collective-permute-start = (f32[130,8,128]{2,1,0:T(8,128)S(1)}, f32[130,8,128]{2,1,0:T(8,128)S(1)}, u32[]{:S(2)}, u32[]{:S(2)}) collective-permute-start(f32[130,8,128]{2,1,0:T(8,128)S(1)} %get-tuple-element.15), channel_id=1, source_target_pairs={{0,8},{8,0},{16,24},{24,16},{32,40},{40,32},{48,56},{56,48},{64,72... | collective-permute-start | bytes 1597448 | tf_op jit(solution)/shard_map/ppermute | solution.py:447
  12.9 13.9 %collective-permute-start.2 = (f32[31,8,128]{2,1,0:T(8,128)S(1)}, f32[31,8,128]{2,1,0:T(8,128)S(1)}, u32[]{:S(2)}, u32[]{:S(2)}) collective-permute-start(f32[31,8,128]{2,1,0:T(8,128)S(1)} %get-tuple-element.17), channel_id=1, source_target_pairs={{0,1},{1,0},{2,3},{3,2},{4,5},{5,4},{6,7},{7,6},{8,9},{9,8},{10,11... | collective-permute-start | bytes 380936 | tf_op jit(solution)/shard_map/ppermute | solution.py:449
  16.1 10.7 %collective-permute-start.4 = (f32[10,8,128]{2,1,0:T(8,128)S(1)}, f32[10,8,128]{2,1,0:T(8,128)S(1)}, u32[]{:S(2)}, u32[]{:S(2)}) collective-permute-start(f32[10,8,128]{2,1,0:T(8,128)S(1)} %get-tuple-element.19), channel_id=1, source_target_pairs={{0,1},{1,0},{2,3},{3,2},{4,5},{5,4},{6,7},{7,6},{8,17},{9,16},{10,... | collective-permute-start | bytes 122888 | tf_op jit(solution)/shard_map/ppermute | solution.py:413
  16.5 10.4 %collective-permute-start.3 = (f32[10,8,128]{2,1,0:T(8,128)S(1)}, f32[10,8,128]{2,1,0:T(8,128)S(1)}, u32[]{:S(2)}, u32[]{:S(2)}) collective-permute-start(f32[10,8,128]{2,1,0:T(8,128)S(1)} %get-tuple-element.18), channel_id=1, source_target_pairs={{0,9},{1,8},{2,11},{3,10},{4,13},{5,12},{6,15},{7,14},{8,1},{9,0},... | collective-permute-start | bytes 122888 | tf_op jit(solution)/shard_map/ppermute | solution.py:413
  27.6 7.6 %collective-permute-start.5 = (f32[424,128]{1,0:T(8,128)S(1)}, f32[424,128]{1,0:T(8,128)S(1)}, u32[]{:S(2)}, u32[]{:S(2)}) collective-permute-start(f32[424,128]{1,0:T(8,128)S(1)} %get-tuple-element.22), channel_id=1, source_target_pairs={{0,2},{2,4},{4,6},{6,0},{1,3},{3,5},{5,7},{7,1},{8,10},{10,12},{12... | collective-permute-start | bytes 651272 | tf_op jit(solution)/shard_map/ppermute | solution.py:460
  28.1 8.4 %collective-permute-start.6 = (f32[424,128]{1,0:T(8,128)S(1)}, f32[424,128]{1,0:T(8,128)S(1)}, u32[]{:S(2)}, u32[]{:S(2)}) collective-permute-start(f32[424,128]{1,0:T(8,128)S(1)} %get-tuple-element.23), channel_id=1, source_target_pairs={{2,0},{4,2},{6,4},{0,6},{3,1},{5,3},{7,5},{1,7},{10,8},{12,10},{14... | collective-permute-start | bytes 651272 | tf_op jit(solution)/shard_map/ppermute | solution.py:461
  43.1 5.2 %collective-permute-start.7 = (f32[8,128]{1,0:T(8,128)S(1)}, f32[8,128]{1,0:T(8,128)S(1)}, u32[]{:S(2)}, u32[]{:S(2)}) collective-permute-start(f32[8,128]{1,0:T(8,128)S(1)} %get-tuple-element.25), channel_id=1, source_target_pairs={{0,1},{1,0},{2,3},{3,2},{4,5},{5,4},{6,7},{7,6},{8,9},{9,8},{10,11... | collective-permute-start | bytes 12296 | tf_op jit(solution)/shard_map/ppermute | solution.py:483

commit v2 on v1

v2 whole, which is shorter than its diff:
```python
import jax
import jax.numpy as jnp
from jax import lax
from jax.experimental import pallas as pl
from jax.experimental.pallas import tpu as pltpu
from jax.sharding import PartitionSpec as P

TILES = 16
PLANES = 8
CORE = TILES * PLANES
CORE_MSG = CORE + 2
EDGE = 10
ROWQ = 10
MESSAGE_ROWS = 424
CHUNK = 5
F32 = jnp.float32
VMEM_LIMIT = 16 * 1024 * 1024
FRONT_LIMIT = 61 * 1024 * 1024
INNER_LIMIT = 16 * 1024 * 1024


def lanes():
    return lax.broadcasted_iota(jnp.int32, (8, 128), 1)


def subs():
    return lax.broadcasted_iota(jnp.int32, (8, 128), 0)


def checker():
    lane = lanes()
    return lax.rem(lane // 64 + lax.rem(lane, 64) + subs(), 2) == 0


def checker_row0(rows):
    lane = lax.broadcasted_iota(jnp.int32, (rows, 128), 1)
    return lax.rem(lane // 64 + lax.rem(lane, 64), 2) == 0


def take(x, index, axis):
    return jnp.take_along_axis(x, index, axis=axis, mode="promise_in_bounds")


def pack_config(spins, thr0, thr1, masks, put):
    mask, flip = masks
    for k in range(TILES):
        for comp in range(3):
            a, b = spins(comp, 0, k), take(spins(comp, 1, k), flip, 0)
            put(comp, k, jnp.where(mask, a, b))
            put(3 + comp, k, jnp.where(mask, b, a))
        a, b = thr0(0, k), take(thr0(1, k), flip, 0)
        put(6, k, (jnp.where(mask, a, b).astype(F32) + 0.5) / 8192.0)
        a, b = thr1(0, k), take(thr1(1, k), flip, 0)
        put(7, k, (jnp.where(mask, b, a).astype(F32) + 0.5) / 8192.0)


def config_reader(spin_buf, thr_buf):
    def spins(comp, half, k):
        return spin_buf[comp, half * 8 : half * 8 + 8, k * 128 : k * 128 + 128]

    def thr(which):
        return lambda half, k: thr_buf[which, half * 8 : half * 8 + 8, k * 128 : k * 128 + 128]

    return spins, thr(0), thr(1)


def edge_message(spins, thr, masks, out, base):
    mask, flip = masks
    low = lanes() < 64
    for comp in range(3):
        own = []
        for side in range(2):
            a, b = spins(side, comp, 0), take(spins(side, comp, 1), flip, 0)
            own.append(jnp.where(mask, a, b))
            out[base + 3 * side + comp] = jnp.where(mask, b, a)
        out[base + 6 + comp] = jnp.where(low, own[0], own[1])
    steps = [jnp.where(mask, thr(side, 0), take(thr(side, 1), flip, 0)) for side in range(2)]
    out[base + 9] = (jnp.where(low, steps[0], steps[1]).astype(F32) + 0.5) / 8192.0


def fetch(spins_ref, thr_ref, config, spin_buf, thr_buf, sem, base):
    copies = [
        pltpu.make_async_copy(spins_ref.at[config], spin_buf, sem.at[base]),
        pltpu.make_async_copy(thr_ref.at[0, config], thr_buf.at[0], sem.at[base + 1]),
        pltpu.make_async_copy(thr_ref.at[1, config], thr_buf.at[1], sem.at[base + 2]),
    ]
    for copy in copies:
        copy.start()
    return copies


def scalars(beta_ref, coup_ref, beta_buf, coup_buf, sem, base):
    copies = [
        pltpu.make_async_copy(beta_ref, beta_buf, sem.at[base]),
        pltpu.make_async_copy(coup_ref, coup_buf, sem.at[base + 1]),
    ]
    for copy in copies:
        copy.start()
    return copies


def front_kernel(
    spins_ref, thr_ref, beta_ref, coup_ref, right_ref, down_ref,
    far_ref, near_ref, far_edge_ref, near_edge_ref, inner_edge_ref,
    edge_spins, edge_thr, spin_buf, thr_buf, right_buf, down_buf, beta_buf, coup_buf, sem,
):
    is_even = lax.rem(lax.axis_index("rep"), 2) == 0
    far, near = jnp.where(is_even, 0, 4), jnp.where(is_even, 4, 0)
    last = TILES - 1
    edge_copies = []
    for side in range(2):
        at = pl.ds(side * last * 128, 128)
        edge_copies.append(
            pltpu.make_async_copy(spins_ref.at[:, :, :, at], edge_spins.at[side], sem.at[side])
        )
        edge_copies.append(
            pltpu.make_async_copy(thr_ref.at[0, :, :, at], edge_thr.at[side], sem.at[2 + side])
        )
    edge_copies.append(pltpu.make_async_copy(right_ref, right_buf, sem.at[4]))
    edge_copies.append(pltpu.make_async_copy(down_ref, down_buf, sem.at[5]))
    for copy in edge_copies:
        copy.start()
    small = scalars(beta_ref, coup_ref, beta_buf, coup_buf, sem, 6)
    leaving = [
        fetch(spins_ref, thr_ref, config, spin_buf.at[n], thr_buf.at[n], sem, 8 + 3 * n)
        for n, config in enumerate((far, near))
    ]
    masks = (checker(), 7 - subs())
    for copy in edge_copies:
        copy.wait()
    bonds = 3 * EDGE
    inner_edge_ref[bonds] = jnp.zeros((8, 128), F32)
    inner_edge_ref[bonds, 0:1] = down_buf[0:1]
    inner_edge_ref[bonds, 1:2] = down_buf[last : last + 1]
    inner_edge_ref[bonds, 2:3] = right_buf[0:1]
    inner_edge_ref[bonds, 3:4] = right_buf[last : last + 1]
    for config, out, base in (
        (1, inner_edge_ref, 0), (2, inner_edge_ref, EDGE), (3, inner_edge_ref, 2 * EDGE),
        (near, near_edge_ref, 0), (far, far_edge_ref, 0),
    ):
        edge_message(
            lambda side, comp, half: edge_spins[side, config, comp, half * 8 : half * 8 + 8],
            lambda side, half: edge_thr[side, config, half * 8 : half * 8 + 8],
            masks, out, base,
        )
    for copy in small:
        copy.wait()
    for n, (config, out) in enumerate(((far, far_ref), (near, near_ref))):
        out[CORE] = jnp.full((8, 128), beta_buf[config], F32)
        out[CORE + 1] = jnp.full((8, 128), coup_buf[config], F32)
        for copy in leaving[n]:
            copy.wait()

        def put(plane, k, value):
            out[k * PLANES + plane] = value

        pack_config(*config_reader(spin_buf.at[n], thr_buf.at[n]), masks, put)


def inner_kernel(
    spins_ref, thr_ref, beta_ref, coup_ref,
    inner_ref, rows_ref, scale_ref,
    spin_buf, thr_buf, beta_buf, coup_buf, sem,
):
    copies = [
        fetch(spins_ref, thr_ref, n + 1, spin_buf.at[n], thr_buf.at[n], sem, 3 * n) for n in range(3)
    ]
    small = scalars(beta_ref, coup_ref, beta_buf, coup_buf, sem, 9)
    masks = (checker(), 7 - subs())
    for n in range(3):
        for copy in copies[n]:
            copy.wait()

        def put(plane, k, value):
            inner_ref[n, k * PLANES + plane] = value
            if plane < 7:
                rows_ref[plane * TILES + k, n : n + 1] = value[0:1]
            if 3 <= plane < 6:
                rows_ref[(plane + 4) * TILES + k, n : n + 1] = value[1:2]

        pack_config(*config_reader(spin_buf.at[n], thr_buf.at[n]), masks, put)
    for copy in small:
        copy.wait()
    sub = subs()
    for base, buf in ((0, beta_buf), (1, coup_buf)):
        scale_ref[base] = jnp.where(sub == 0, buf[1], jnp.where(sub == 1, buf[2], buf[3]))


def slices_kernel(
    rows_ref, scale_ref, x_ref, y_ref, inner_edge_ref, x_edge_ref, y_edge_ref,
    up_ref, down_ref, own_ref,
):
    sub = subs()
    even = checker_row0(8)
    low = lanes() < 64
    swap = jnp.bitwise_xor(lanes(), 1)

    def five(mine, x, y):
        return jnp.where(sub == 3, x, jnp.where(sub == 4, y, mine))

    def row(q, k):
        plane, s = (q, 0) if q < 7 else (q - 4, 1)
        at = k * PLANES + plane
        return five(rows_ref[q * TILES + k], x_ref[at, s : s + 1], y_ref[at, s : s + 1])

    for k in range(TILES):
        p0 = [row(c, k) for c in range(3)]
        p1 = [row(3 + c, k) for c in range(3)]
        w0 = row(6, k)
        second = [row(7 + c, k) for c in range(3)]
        for c in range(3):
            own_ref[k * 3 + c] = p1[c]
        swapped_y, swapped_w = take(second[1], swap, 1), take(w0, swap, 1)
        down = [jnp.where(even, p0[c], p1[c]) for c in range(3)]
        down += [jnp.where(even, second[0], swapped_y), jnp.where(even, second[2], swapped_w)]
        up = [jnp.where(even, p1[c], p0[c]) for c in range(3)]
        up += [jnp.where(even, swapped_y, second[0]), jnp.where(even, swapped_w, second[2])]
        for q in range(CHUNK):
            at = (k * CHUNK + q) * 5
            down_ref[at : at + 5] = down[q][0:5]
            up_ref[at : at + 5] = up[q][0:5]
    for c in range(3):
        merged = []
        for ref, base in ((inner_edge_ref, 0), (inner_edge_ref, EDGE), (inner_edge_ref, 2 * EDGE), (x_edge_ref, 0), (y_edge_ref, 0)):
            merged.append(jnp.where(low[0:1], ref[base + c, 0:1], ref[base + 3 + c, 0:1]))
        corner = five(
            jnp.where(sub == 0, merged[0], jnp.where(sub == 1, merged[1], merged[2])), merged[3], merged[4]
        )
        at = (TILES * CHUNK + c) * 5
        down_ref[at : at + 5] = corner[0:5]
        up_ref[at : at + 5] = corner[0:5]
    at = (TILES * CHUNK + 3) * 5
    down_ref[at:MESSAGE_ROWS] = jnp.zeros((MESSAGE_ROWS - at, 128), F32)
    up_ref[at:MESSAGE_ROWS] = jnp.zeros((MESSAGE_ROWS - at, 128), F32)
    for base in range(2):
        own_ref[3 * TILES + base] = five(scale_ref[base], x_ref[CORE + base], y_ref[CORE + base])


def row_neighbours():
    lane = lanes()
    column = lax.rem(lane, 64)
    right = jnp.where(column == 63, lane - 63, lane + 1)
    left = jnp.where(column == 0, lane + 63, lane - 1)
    return right, left


def normalized(moved):
    scale = lax.rsqrt(0.25 + (moved[0] * moved[0] + moved[1] * moved[1] + moved[2] * moved[2]))
    return [m * scale for m in moved]


def edge_list(inner_edge_ref, x_edge_ref, y_edge_ref):
    inner = [(inner_edge_ref, n * EDGE) for n in range(3)]
    return inner + [(x_edge_ref, 0), (y_edge_ref, 0)]


def core_list(inner_ref, x_ref, y_ref):
    return [inner_ref.at[0], inner_ref.at[1], inner_ref.at[2], x_ref, y_ref]


def space_field(bonds, at, above, here, turned, below, masks):
    low, right_at, left_at = masks
    return (
        bonds[at * 4] * jnp.where(low, turned, below)
        + bonds[at * 4 + 1] * jnp.where(low, above, turned)
        + bonds[at * 4 + 2] * take(here, right_at, 1)
        + bonds[at * 4 + 3] * take(here, left_at, 1)
    )


def turn(x):
    return pltpu.roll(x, 64, 1)


def prepare_kernel(
    inner_ref, x_ref, y_ref, inner_edge_ref, x_edge_ref, y_edge_ref, own_ref, right_ref, bdown_ref,
    moved_ref, bonds,
):
    low = lanes() < 64
    sub = subs()
    right_at, left_at = row_neighbours()
    masks = (low, right_at, left_at)
    edge_bonds = 3 * EDGE

    def bond_rows(k):
        if k == -1:
            return inner_edge_ref[edge_bonds, 1:2], inner_edge_ref[edge_bonds, 3:4]
        if k == TILES:
            return inner_edge_ref[edge_bonds, 0:1], inner_edge_ref[edge_bonds, 2:3]
        return bdown_ref[k : k + 1], right_ref[k : k + 1]

    before = jnp.zeros((8, 128), F32)
    for k in range(-1, TILES + 1):
        down, right = (jnp.broadcast_to(row, (8, 128)) for row in bond_rows(k))
        turned = turn(down)
        bonds[(k + 1) * 4] = down
        bonds[(k + 1) * 4 + 1] = jnp.where(low, before, turned)
        bonds[(k + 1) * 4 + 2] = right
        bonds[(k + 1) * 4 + 3] = take(right, left_at, 1)
        before = turned

    edges = edge_list(inner_edge_ref, x_edge_ref, y_edge_ref)
    for n, core in enumerate(core_list(inner_ref, x_ref, y_ref)):
        edge, base = edges[n]
        beta = jnp.broadcast_to(own_ref[3 * TILES, n : n + 1], (8, 128))
        coup = jnp.broadcast_to(own_ref[3 * TILES + 1, n : n + 1], (8, 128))

        def second(at, c):
            if at == 0:
                return edge[base + 3 + c]
            if at == TILES + 1:
                return edge[base + c]
            return core[(at - 1) * PLANES + 3 + c]

        here = [second(0, c) for c in range(3)]
        turned = [turn(x) for x in here]
        above = turned
        for at in range(TILES + 2):
            outer = at == 0 or at == TILES + 1
            if at <= TILES:
                following = [second(at + 1, c) for c in range(3)]
                below = [turn(x) for x in following]
            else:
                following, below = here, turned
            weight = edge[base + 9] if outer else core[(at - 1) * PLANES + 6]
            for c in range(3):
                x = here[c]
                space = space_field(bonds, at, above[c], x, turned[c], below[c], masks)
                inside = jnp.where(sub == 0, 0.0, pltpu.roll(x, 1, 0)) + jnp.where(sub == 7, x, pltpu.roll(x, 7, 0))
                mine = edge[base + 6 + c] if outer else core[(at - 1) * PLANES + c]
                moved_ref[n, at * 3 + c] = mine + weight * (beta * space + coup * inside)
            above, turned, here = turned, below, following


def sweep_kernel(
    inner_ref, x_ref, y_ref, inner_edge_ref, x_edge_ref, y_edge_ref, own_ref, moved_ref, bonds, up_ref, down_ref,
    partner_ref, accept_ref,
    final_ref, energy_ref,
    halo, halo_first,
):
    rep = lax.axis_index("rep")
    is_even = lax.rem(rep, 2) == 0
    low = lanes() < 64
    sub = subs()
    lane = lanes()
    mask = checker()
    right_at, left_at = row_neighbours()
    masks = (low, right_at, left_at)

    even8 = checker_row0(8)
    swap = jnp.bitwise_xor(lanes(), 1)

    def chunk(ref, i):
        at = i * 5
        return ref[at : at + 8]

    beta_rows = own_ref[3 * TILES]
    coup_rows = own_ref[3 * TILES + 1]
    for k in range(TILES):
        for c in range(3):
            up, down = chunk(up_ref, k * CHUNK + c), chunk(down_ref, k * CHUNK + c)
            halo[(k + 1) * 3 + c] = jnp.where(even8, up, down)
            halo_first[k * 3 + c] = jnp.where(even8, down, up)
    for c in range(3):
        corner = jnp.where(even8, chunk(up_ref, TILES * CHUNK + c), chunk(down_ref, TILES * CHUNK + c))
        halo[c] = corner
        halo[(TILES + 1) * 3 + c] = corner
    here = [halo[3 + c] for c in range(3)]
    above, turned = [turn(halo[c]) for c in range(3)], [turn(x) for x in here]
    for k in range(TILES):
        following = [halo[(k + 2) * 3 + c] for c in range(3)]
        below = [turn(x) for x in following]
        a_up, a_down = chunk(up_ref, k * CHUNK + 3), chunk(down_ref, k * CHUNK + 3)
        b_up, b_down = chunk(up_ref, k * CHUNK + 4), chunk(down_ref, k * CHUNK + 4)
        second = [
            jnp.where(even8, a_down, a_up),
            take(jnp.where(even8, a_up, a_down), swap, 1),
            jnp.where(even8, b_down, b_up),
        ]
        weight = take(jnp.where(even8, b_up, b_down), swap, 1)
        moved = []
        for c in range(3):
            field = beta_rows * space_field(bonds, k + 1, above[c], here[c], turned[c], below[c], masks)
            field = field + coup_rows * (own_ref[k * 3 + c] + second[c])
            moved.append(halo_first[k * 3 + c] + weight * field)
        fresh = normalized(moved)
        for c in range(3):
            halo_first[k * 3 + c] = fresh[c]
        above, turned, here = turned, below, following

    edges = edge_list(inner_edge_ref, x_edge_ref, y_edge_ref)
    energy_ref[...] = jnp.zeros((8, 128), F32)
    for n, core in enumerate(core_list(inner_ref, x_ref, y_ref)):
        edge, base = edges[n]
        beta = jnp.broadcast_to(own_ref[3 * TILES, n : n + 1], (8, 128))
        coup = jnp.broadcast_to(own_ref[3 * TILES + 1, n : n + 1], (8, 128))
        coup_outer = jnp.where(sub == 0, coup, 0.0)
        if n < 3:
            slot = n + 1
        elif n == 3:
            slot = jnp.where(is_even, 4, 0)
        else:
            slot = jnp.where(is_even, 0, 4)
        target = jnp.where(accept_ref[slot] == 1, jnp.clip(partner_ref[slot] - 5 * rep, 0, 4), slot)

        def pass_0(at):
            outer = at == 0 or at == TILES + 1
            factor = (edge[base + 9] if outer else core[(at - 1) * PLANES + 6]) * coup_outer
            fresh = normalized([
                moved_ref[n, at * 3 + c] + factor * halo[at * 3 + c, n : n + 1] for c in range(3)
            ])
            if not outer:
                for c in range(3):
                    final_ref[target, (at - 1) * 6 + c] = fresh[c]
            return fresh, [turn(x) for x in fresh]

        _, above = pass_0(0)
        here, turned = pass_0(1)
        total = jnp.zeros((8, 128), F32)
        for k in range(TILES):
            following, below = pass_0(k + 2)
            weight = core[k * PLANES + 7]
            fields, moved = [], []
            for c in range(3):
                x = here[c]
                space = space_field(bonds, k + 1, above[c], x, turned[c], below[c], masks)
                outside = halo_first[k * 3 + c, n : n + 1]
                around = jnp.where(sub == 0, outside, pltpu.roll(x, 1, 0)) + jnp.where(sub == 7, x, pltpu.roll(x, 7, 0))
                moved.append(core[k * PLANES + 3 + c] + weight * (beta * space + coup * around))
                fields.append(space)
            fresh = normalized(moved)
            total = total + (fresh[0] * fields[0] + fresh[1] * fields[1] + fresh[2] * fields[2])
            for c in range(3):
                final_ref[target, k * 6 + 3 + c] = fresh[c]
            above, turned, here = turned, below, following
        head = jnp.sum(jnp.where(mask, 0.0, total), axis=1, keepdims=True)
        back = jnp.sum(jnp.where(mask, total, 0.0), axis=1, keepdims=True)
        line = jnp.where(lane == sub, head, 0.0) + jnp.where(lane == 15 - sub, back, 0.0)
        line = jnp.sum(line, axis=0, keepdims=True)
        energy_ref[...] = jnp.where(sub == target, -line / 4096.0, energy_ref[...])


def unpack_kernel(final_ref, out_ref, out_buf, sem):
    mask = checker()
    flip = 7 - subs()
    writes = []
    for n in range(5):
        for k in range(TILES):
            for c in range(3):
                p0, p1 = final_ref[n, k * 6 + c], final_ref[n, k * 6 + 3 + c]
                out_buf[n, c, 0:8, k * 128 : k * 128 + 128] = jnp.where(mask, p0, p1)
                out_buf[n, c, 8:16, k * 128 : k * 128 + 128] = take(jnp.where(mask, p1, p0), flip, 0)
        write = pltpu.make_async_copy(out_buf.at[n], out_ref.at[n], sem.at[n])
        write.start()
        writes.append(write)
    for write in writes:
        write.wait()


def params(limit=VMEM_LIMIT):
    return pltpu.CompilerParams(vmem_limit_bytes=limit)


def vmem():
    return pl.BlockSpec(memory_space=pltpu.VMEM)


def smem():
    return pl.BlockSpec(memory_space=pltpu.SMEM)


def hbm():
    return pl.BlockSpec(memory_space=pltpu.HBM)


def anywhere():
    return pl.BlockSpec(memory_space=pl.ANY)


def shape(*dims):
    return jax.ShapeDtypeStruct(dims, F32)


def on_device(spins, bond_right, bond_down, betas, time_coupling, thresholds, partner, accept):
    ranks, depth = lax.axis_size("rep"), lax.axis_size("tm")
    axes = ("rep", "tm", "space")
    right, down = bond_right.reshape(TILES, 128), bond_down.reshape(TILES, 128)

    def far_of(r):
        other = r - 1 if r % 2 == 0 else r + 1
        return other if 0 <= other < ranks else r

    def near_of(r):
        return r + 1 if r % 2 == 0 else r - 1

    def crosswise(x, of):
        pairs = [
            ((r * depth + t) * 2 + s, (of(r) * depth + t) * 2 + 1 - s)
            for r in range(ranks) for t in range(depth) for s in range(2)
        ]
        return lax.ppermute(x, axes, pairs)

    far_core, near_core, far_edge, near_edge, inner_edge = pl.pallas_call(
        front_kernel,
        out_shape=(
            shape(CORE_MSG, 8, 128), shape(CORE_MSG, 8, 128),
            shape(EDGE, 8, 128), shape(EDGE, 8, 128), shape(3 * EDGE + 1, 8, 128),
        ),
        in_specs=[hbm()] * 6,
        out_specs=(vmem(),) * 5,
        scratch_shapes=[
            pltpu.VMEM((2, 5, 3, 16, 128), F32),
            pltpu.VMEM((2, 5, 16, 128), jnp.int32),
            pltpu.VMEM((2, 3, 16, 2048), F32),
            pltpu.VMEM((2, 2, 16, 2048), jnp.int32),
            pltpu.VMEM((TILES, 128), F32),
            pltpu.VMEM((TILES, 128), F32),
            pltpu.SMEM((5,), F32),
            pltpu.SMEM((5,), F32),
            pltpu.SemaphoreType.DMA((14,)),
        ],
        compiler_params=params(FRONT_LIMIT),
        name="front",
    )(spins, thresholds, betas, time_coupling, right, down)
    far_core = lax.ppermute(far_core, "rep", [(r, far_of(r)) for r in range(ranks)])
    inner_edge = lax.ppermute(inner_edge, "space", [(0, 1), (1, 0)])
    far_edge = crosswise(far_edge, far_of)
    near_edge = crosswise(near_edge, near_of)
    near_core = lax.ppermute(near_core, "rep", [(r, near_of(r)) for r in range(ranks)])

    inner, rows, scale = pl.pallas_call(
        inner_kernel,
        out_shape=(shape(3, CORE, 8, 128), shape(ROWQ * TILES, 8, 128), shape(2, 8, 128)),
        in_specs=[hbm()] * 4,
        out_specs=(vmem(),) * 3,
        scratch_shapes=[
            pltpu.VMEM((3, 3, 16, 2048), F32),
            pltpu.VMEM((3, 2, 16, 2048), jnp.int32),
            pltpu.SMEM((5,), F32),
            pltpu.SMEM((5,), F32),
            pltpu.SemaphoreType.DMA((11,)),
        ],
        compiler_params=params(INNER_LIMIT),
        name="pack_inner",
    )(spins, thresholds, betas, time_coupling)

    message = shape(MESSAGE_ROWS, 128)
    up, down_msg, own = pl.pallas_call(
        slices_kernel,
        out_shape=(message, message, shape(3 * TILES + 2, 8, 128)),
        in_specs=[vmem()] * 7,
        out_specs=(vmem(),) * 3,
        compiler_params=params(),
        name="slices",
    )(rows, scale, near_core, far_core, inner_edge, near_edge, far_edge)
    from_before = lax.ppermute(up, "tm", [(t, (t + 1) % depth) for t in range(depth)])
    from_after = lax.ppermute(down_msg, "tm", [((t + 1) % depth, t) for t in range(depth)])

    edges = (inner_edge, near_edge, far_edge)
    moved, bonds = pl.pallas_call(
        prepare_kernel,
        out_shape=(shape(5, (TILES + 2) * 3, 8, 128), shape((TILES + 2) * 4, 8, 128)),
        in_specs=[vmem()] * 9,
        out_specs=(vmem(),) * 2,
        compiler_params=params(),
        name="prepare",
    )(inner, near_core, far_core, *edges, own, right, down)
    final, energy = pl.pallas_call(
        sweep_kernel,
        out_shape=(shape(5, TILES * 6, 8, 128), shape(8, 128)),
        in_specs=[vmem()] * 11 + [smem()] * 2,
        out_specs=(vmem(),) * 2,
        scratch_shapes=[
            pltpu.VMEM(((TILES + 2) * 3, 8, 128), F32),
            pltpu.VMEM((TILES * 3, 8, 128), F32),
        ],
        compiler_params=params(),
        name="sweep",
    )(
        inner, near_core, far_core, *edges, own, moved, bonds, from_before, from_after, partner, accept,
    )
    other_energy = lax.ppermute(energy, "space", [(0, 1), (1, 0)])
    swapped = pl.pallas_call(
        unpack_kernel,
        out_shape=shape(5, 3, 16, 2048),
        in_specs=[vmem()],
        out_specs=hbm(),
        scratch_shapes=[pltpu.VMEM((5, 3, 16, 2048), F32), pltpu.SemaphoreType.DMA((5,))],
        compiler_params=params(),
        name="unpack",
    )(final)
    energy = energy + other_energy
    return swapped, energy[:5, :16]


def solution(mesh):
    placed = (
        P("rep", None, "tm", "space"),
        P("space"),
        P("space"),
        P("rep"),
        P("rep"),
        P(None, "rep", "tm", "space"),
        P("rep"),
        P("rep"),
    )
    return jax.shard_map(
        on_device,
        mesh=mesh,
        in_specs=placed,
        out_specs=(P("rep", None, "tm", "space"), P("rep", "tm")),
        check_vma=False,
    )
```

time: 49.1 us -> 39.4 us (0.80)
  waiting for transfers between devices: 17.7 us -> 12 us
  local copies, waits for them, and re-layouts: 4.19 us -> 1.34 us
  starting transfers between devices: 14.4 us -> 13.8 us
  Pallas kernels: 11.2 us -> 10.7 us
    ppermute x1, starting transfers between devices: 3.33 us -> 0.09 us  [on_device(): lax.ppermute(near_core, 'rep', [(r, near_of(r)) for r in range(ranks)])]
    unnamed x18 -> x16, local copies, waits for them, and re-layouts: 4.19 us -> 1.34 us
    ppermute x1, waiting for transfers between devices: 4.78 us -> 2.23 us  [on_device(): other_energy = lax.ppermute(energy, 'space', [(0, 1), (1, 0)])]
    ppermute x1, waiting for transfers between devices: 5.47 us -> 3.19 us  [on_device(): lax.ppermute(up, 'tm', [(t, (t + 1) % depth) for t in range(depth)])]
    ppermute x1, starting transfers between devices: 0.42 us -> 1.57 us  [on_device(): other_energy = lax.ppermute(energy, 'space', [(0, 1), (1, 0)])]
    ppermute x1, starting transfers between devices: 0.69 us -> 1.7 us  [on_device(): lax.ppermute(far_core, 'rep', [(r, far_of(r)) for r in range(ranks)])]
    ppermute x2, waiting for transfers between devices: 6.08 us -> 5.21 us  [crosswise(): return lax.ppermute(x, axes, pairs)]
    ppermute x2, starting transfers between devices: 4.6 us -> 5.19 us  [crosswise(): return lax.ppermute(x, axes, pairs)]
  transfers between devices with their start and end apart: 8 -> 8, of which waited for: 4 -> 5; matrix products, arithmetic and copies ran while one was open for 0% -> 0% of each run, Pallas kernels for 6% -> 13%
where the time goes in v2:
time: 39.4 us; the launch traced here: 39.3 us
  starting transfers between devices  13.8 us (35%)
  waiting for transfers between devices  12 us (30%)
  Pallas kernels  10.7 us (27%)
  local copies, waits for them, and re-layouts  1.34 us (3%)
  between operations  0.73 us (2%)
  other arithmetic  0.6 us (2%)
    ppermute x2, waiting for transfers between devices, crosswise(): return lax.ppermute(x, axes, pairs)  5.21 us
    ppermute x2, starting transfers between devices, crosswise(): return lax.ppermute(x, axes, pairs)  5.19 us
    ppermute x1, starting transfers between devices, on_device(): inner_edge = lax.ppermute(inner_edge, 'space', [(0, 1), (1, 0)])  3.19 us
    ppermute x1, waiting for transfers between devices, on_device(): lax.ppermute(up, 'tm', [(t, (t + 1) % depth) for t in range(depth)])  3.19 us
    pallas_call x1, Pallas kernels, on_device(): pl.pallas_call(sweep_kernel, out_shape=(shape(5, TILES * 6, 8, 128), shap...  2.78 us
    pallas_call x1, Pallas kernels, on_device(): pl.pallas_call(front_kernel, out_shape=(shape(CORE_MSG, 8, 128), shape(CO...  2.77 us
    ppermute x1, waiting for transfers between devices, on_device(): other_energy = lax.ppermute(energy, 'space', [(0, 1), (1, 0)])  2.23 us
    pallas_call x1, Pallas kernels, on_device(): pl.pallas_call(inner_kernel, out_shape=(shape(3, CORE, 8, 128), shape(ROW...  2.22 us
  transfers between devices with their start and end apart: 8, of which 5 were waited for; matrix products, arithmetic and copies ran while one was open for 0% of the time, Pallas kernels for 13%

profile of v2, /device:TPU:6, one launch (start us, length us, event | category | flops | bytes accessed | tf_op | source)
XLA Modules:
  0.0 39.3 jit_solution(11708361503098718991)
XLA Ops:
  0.6 0.0 copy-start.5
  0.6 0.0 copy-start.4
  0.6 0.0 copy-start
  0.7 2.8 %front.1 = (f32[130,8,128]{2,1,0:T(8,128)}, f32[130,8,128]{2,1,0:T(8,128)}, f32[10,8,128]{2,1,0:T(8,128)}, f32[10,8,128]{2,1,0:T(8,128)}, f32[31,8,128]{2,1,0:T(8,128)}) custom-call(f32[5,3,16,2048]{3,2,1,0:T(8,128)} %spins_ref.3, s32[2,5,16,2048]{3,2,1,0:T(8,128)} %thr_ref.3, f32[5]{0:T(128)} %beta_ref.3, f32[5]{0:T(128)} %coup_ref.3, f32[16,128]{1,0:T(8,128)} %bitcast.3, ...), custom_call_target="tpu_custom_call" | custom-call | tf_op jit(solution)/shard_map/front/pallas_call | solution.py:503
  3.4 0.1 collective-permute-start
  3.5 1.7 %collective-permute-start.1 = (f32[130,8,128]{2,1,0:T(8,128)}, f32[130,8,128]{2,1,0:T(8,128)S(1)}, u32[]{:S(2)}, u32[]{:S(2)}) collective-permute-start(f32[130,8,128]{2,1,0:T(8,128)} %get-tuple-element.19), channel_id=1, source_target_pairs={{0,0},{8,16},{16,8},{24,32},{32,24},{40,48},{48,40},{56,64},{64,56... | collective-permute-start | bytes 1597448 | tf_op jit(solution)/shard_map/ppermute | solution.py:525
  5.2 3.2 %collective-permute-start.2 = (f32[31,8,128]{2,1,0:T(8,128)}, f32[31,8,128]{2,1,0:T(8,128)S(1)}, u32[]{:S(2)}, u32[]{:S(2)}) collective-permute-start(f32[31,8,128]{2,1,0:T(8,128)} %get-tuple-element.20), channel_id=1, source_target_pairs={{0,1},{1,0},{2,3},{3,2},{4,5},{5,4},{6,7},{7,6},{8,9},{9,8},{10,11... | collective-permute-start | bytes 380936 | tf_op jit(solution)/shard_map/ppermute | solution.py:526
  8.4 2.0 %collective-permute-start.3 = (f32[10,8,128]{2,1,0:T(8,128)}, f32[10,8,128]{2,1,0:T(8,128)S(1)}, u32[]{:S(2)}, u32[]{:S(2)}) collective-permute-start(f32[10,8,128]{2,1,0:T(8,128)} %get-tuple-element.21), channel_id=1, source_target_pairs={{0,9},{1,8},{2,11},{3,10},{4,13},{5,12},{6,15},{7,14},{8,1},{9,0},... | collective-permute-start | bytes 122888 | tf_op jit(solution)/shard_map/ppermute | solution.py:501
  10.5 3.2 %collective-permute-start.4 = (f32[10,8,128]{2,1,0:T(8,128)}, f32[10,8,128]{2,1,0:T(8,128)S(1)}, u32[]{:S(2)}, u32[]{:S(2)}) collective-permute-start(f32[10,8,128]{2,1,0:T(8,128)} %get-tuple-element.22), channel_id=1, source_target_pairs={{0,1},{1,0},{2,3},{3,2},{4,5},{5,4},{6,7},{7,6},{8,17},{9,16},{10,... | collective-permute-start | bytes 122888 | tf_op jit(solution)/shard_map/ppermute | solution.py:501
  13.6 0.0 copy-done.5
  13.6 0.0 copy-done.4
  13.6 1.3 %copy-done.1 = s32[2,5,16,2048]{3,2,1,0:T(8,128)S(1)} copy-done((s32[2,5,16,2048]{3,2,1,0:T(8,128)S(1)}, s32[2,5,16,2048]{3,2,1,0:T(8,128)}, u32[]{:S(2)}) %copy-start.1) | copy-done | bytes 1310744
  15.0 2.2 %pack_inner.1 = (f32[3,128,8,128]{3,2,1,0:T(8,128)S(1)}, f32[160,8,128]{2,1,0:T(8,128)S(1)}, f32[2,8,128]{2,1,0:T(8,128)S(1)}) custom-call(f32[5,3,16,2048]{3,2,1,0:T(8,128)S(1)} %copy-done, s32[2,5,16,2048]{3,2,1,0:T(8,128)S(1)} %copy-done.1, f32[5]{0:T(128)S(1)} %copy-done.4, f32[5]{0:T(128)S(1)} %copy-done.5), custom_call_target="tpu_custom_call" | custom-call | tf_op jit(solution)/shard_map/pack_inner/pallas_call | solution.py:531
  17.2 1.5 %collective-permute-done.3.x_edge_ref = f32[10,8,128]{2,1,0:T(8,128)S(1)} collective-permute-done((f32[10,8,128]{2,1,0:T(8,128)}, f32[10,8,128]{2,1,0:T(8,128)S(1)}, u32[]{:S(2)}, u32[]{:S(2)}) %collective-permute-start.3) | collective-permute-done | bytes 40992 | tf_op jit(solution)/shard_map/ppermute | solution.py:501
  18.7 3.7 %collective-permute-done.4.y_edge_ref = f32[10,8,128]{2,1,0:T(8,128)S(1)} collective-permute-done((f32[10,8,128]{2,1,0:T(8,128)}, f32[10,8,128]{2,1,0:T(8,128)S(1)}, u32[]{:S(2)}, u32[]{:S(2)}) %collective-permute-start.4) | collective-permute-done | bytes 40992 | tf_op jit(solution)/shard_map/ppermute | solution.py:501
  22.4 0.0 collective-permute-done.2.inner_edge_ref
  22.4 0.0 collective-permute-done.x_ref
  22.4 0.0 collective-permute-done.1.y_ref
  22.4 0.2 slices.1
  22.6 0.0 copy-start.6
  22.6 0.0 copy-start.7
  22.6 0.6 %collective-permute-start.5 = (f32[424,128]{1,0:T(8,128)S(1)}, f32[424,128]{1,0:T(8,128)S(1)}, u32[]{:S(2)}, u32[]{:S(2)}) collective-permute-start(f32[424,128]{1,0:T(8,128)S(1)} %get-tuple-element.28), channel_id=1, source_target_pairs={{0,2},{2,4},{4,6},{6,0},{1,3},{3,5},{5,7},{7,1},{8,10},{10,12},{12... | collective-permute-start | bytes 651272 | tf_op jit(solution)/shard_map/ppermute | solution.py:556
  23.2 1.5 %collective-permute-start.6 = (f32[424,128]{1,0:T(8,128)S(1)}, f32[424,128]{1,0:T(8,128)S(1)}, u32[]{:S(2)}, u32[]{:S(2)}) collective-permute-start(f32[424,128]{1,0:T(8,128)S(1)} %get-tuple-element.29), channel_id=1, source_target_pairs={{2,0},{4,2},{6,4},{0,6},{3,1},{5,3},{7,5},{1,7},{10,8},{12,10},{14... | collective-permute-start | bytes 651272 | tf_op jit(solution)/shard_map/ppermute | solution.py:557
  24.7 1.4 %prepare.1 = (f32[5,54,8,128]{3,2,1,0:T(8,128)S(1)}, f32[72,8,128]{2,1,0:T(8,128)S(1)}) custom-call(f32[3,128,8,128]{3,2,1,0:T(8,128)S(1)} %get-tuple-element.17.inner_ref, f32[130,8,128]{2,1,0:T(8,128)S(1)} %collective-permute-done.x_ref, f32[130,8,128]{2,1,0:T(8,128)S(1)} %collective-permute-done.1.y_ref, ...), custom_call_target="tpu_custom_call" | custom-call | tf_op jit(solution)/shard_map/prepare/pallas_call | solution.py:560
  26.1 3.2 %collective-permute-done.5.up_ref = f32[424,128]{1,0:T(8,128)S(1)} collective-permute-done((f32[424,128]{1,0:T(8,128)S(1)}, f32[424,128]{1,0:T(8,128)S(1)}, u32[]{:S(2)}, u32[]{:S(2)}) %collective-permute-start.5) | collective-permute-done | bytes 217120 | tf_op jit(solution)/shard_map/ppermute | solution.py:556
  29.3 1.4 %collective-permute-done.6.down_ref = f32[424,128]{1,0:T(8,128)S(1)} collective-permute-done((f32[424,128]{1,0:T(8,128)S(1)}, f32[424,128]{1,0:T(8,128)S(1)}, u32[]{:S(2)}, u32[]{:S(2)}) %collective-permute-start.6) | collective-permute-done | bytes 217120 | tf_op jit(solution)/shard_map/ppermute | solution.py:557
  30.7 0.0 copy-done.6
  30.7 2.8 %sweep.1 = (f32[5,96,8,128]{3,2,1,0:T(8,128)S(1)}, f32[8,128]{1,0:T(8,128)S(1)}) custom-call(f32[3,128,8,128]{3,2,1,0:T(8,128)S(1)} %get-tuple-element.17.inner_ref, f32[130,8,128]{2,1,0:T(8,128)S(1)} %collective-permute-done.x_ref, f32[130,8,128]{2,1,0:T(8,128)S(1)} %collective-permute-done.1.y_ref, ...), custom_call_target="tpu_custom_call" | custom-call | tf_op jit(solution)/shard_map/sweep/pallas_call | solution.py:568
  33.5 1.6 %collective-permute-start.7 = (f32[8,128]{1,0:T(8,128)S(1)}, f32[8,128]{1,0:T(8,128)S(1)}, u32[]{:S(2)}, u32[]{:S(2)}) collective-permute-start(f32[8,128]{1,0:T(8,128)S(1)} %get-tuple-element.31), channel_id=1, source_target_pairs={{0,1},{1,0},{2,3},{3,2},{4,5},{5,4},{6,7},{7,6},{8,9},{9,8},{10,11... | collective-permute-start | bytes 12296 | tf_op jit(solution)/shard_map/ppermute | solution.py:582
  35.1 1.3 %unpack.1 = f32[5,3,16,2048]{3,2,1,0:T(8,128)} custom-call(f32[5,96,8,128]{3,2,1,0:T(8,128)S(1)} %get-tuple-element.30.final_ref), custom_call_target="tpu_custom_call" | custom-call | tf_op jit(solution)/shard_map/unpack/pallas_call | solution.py:583
  36.4 2.2 %collective-permute-done.7 = f32[8,128]{1,0:T(8,128)S(1)} collective-permute-done((f32[8,128]{1,0:T(8,128)S(1)}, f32[8,128]{1,0:T(8,128)S(1)}, u32[]{:S(2)}, u32[]{:S(2)}) %collective-permute-start.7) | collective-permute-done | bytes 4128 | tf_op jit(solution)/shard_map/ppermute | solution.py:582
  38.7 0.6 %add.3 = f32[8,128]{1,0:T(8,128)} add(f32[8,128]{1,0:T(8,128)S(1)} %get-tuple-element.31, f32[8,128]{1,0:T(8,128)S(1)} %collective-permute-done.7) | non-fusion elementwise | flops 1024 | bytes 12288 | tf_op jit(solution)/shard_map/add | solution.py:592
  (7 shorter events, 0.0 us)
Async XLA Ops:
  0.6 13.0 %copy-start.5 = (f32[5]{0:T(128)S(1)}, f32[5]{0:T(128)}, u32[]{:S(2)}) copy-start(f32[5]{0:T(128)} %coup_ref.3) | copy-start | bytes 64
  0.6 13.0 %copy-start.4 = (f32[5]{0:T(128)S(1)}, f32[5]{0:T(128)}, u32[]{:S(2)}) copy-start(f32[5]{0:T(128)} %beta_ref.3) | copy-start | bytes 64
  0.6 13.0 %copy-start = (f32[5,3,16,2048]{3,2,1,0:T(8,128)S(1)}, f32[5,3,16,2048]{3,2,1,0:T(8,128)}, u32[]{:S(2)}) copy-start(f32[5,3,16,2048]{3,2,1,0:T(8,128)} %spins_ref.3) | copy-start | bytes 5898244
  3.4 19.0 %collective-permute-start = (f32[130,8,128]{2,1,0:T(8,128)}, f32[130,8,128]{2,1,0:T(8,128)S(1)}, u32[]{:S(2)}, u32[]{:S(2)}) collective-permute-start(f32[130,8,128]{2,1,0:T(8,128)} %get-tuple-element.18), channel_id=1, source_target_pairs={{0,8},{8,0},{16,24},{24,16},{32,40},{40,32},{48,56},{56,48},{64,72... | collective-permute-start | bytes 1597448 | tf_op jit(solution)/shard_map/ppermute | solution.py:529
  3.5 18.9 %collective-permute-start.1 = (f32[130,8,128]{2,1,0:T(8,128)}, f32[130,8,128]{2,1,0:T(8,128)S(1)}, u32[]{:S(2)}, u32[]{:S(2)}) collective-permute-start(f32[130,8,128]{2,1,0:T(8,128)} %get-tuple-element.19), channel_id=1, source_target_pairs={{0,0},{8,16},{16,8},{24,32},{32,24},{40,48},{48,40},{56,64},{64,56... | collective-permute-start | bytes 1597448 | tf_op jit(solution)/shard_map/ppermute | solution.py:525
  5.2 17.2 %collective-permute-start.2 = (f32[31,8,128]{2,1,0:T(8,128)}, f32[31,8,128]{2,1,0:T(8,128)S(1)}, u32[]{:S(2)}, u32[]{:S(2)}) collective-permute-start(f32[31,8,128]{2,1,0:T(8,128)} %get-tuple-element.20), channel_id=1, source_target_pairs={{0,1},{1,0},{2,3},{3,2},{4,5},{5,4},{6,7},{7,6},{8,9},{9,8},{10,11... | collective-permute-start | bytes 380936 | tf_op jit(solution)/shard_map/ppermute | solution.py:526
  8.4 10.3 %collective-permute-start.3 = (f32[10,8,128]{2,1,0:T(8,128)}, f32[10,8,128]{2,1,0:T(8,128)S(1)}, u32[]{:S(2)}, u32[]{:S(2)}) collective-permute-start(f32[10,8,128]{2,1,0:T(8,128)} %get-tuple-element.21), channel_id=1, source_target_pairs={{0,9},{1,8},{2,11},{3,10},{4,13},{5,12},{6,15},{7,14},{8,1},{9,0},... | collective-permute-start | bytes 122888 | tf_op jit(solution)/shard_map/ppermute | solution.py:501
  10.5 11.9 %collective-permute-start.4 = (f32[10,8,128]{2,1,0:T(8,128)}, f32[10,8,128]{2,1,0:T(8,128)S(1)}, u32[]{:S(2)}, u32[]{:S(2)}) collective-permute-start(f32[10,8,128]{2,1,0:T(8,128)} %get-tuple-element.22), channel_id=1, source_target_pairs={{0,1},{1,0},{2,3},{3,2},{4,5},{5,4},{6,7},{7,6},{8,17},{9,16},{10,... | collective-permute-start | bytes 122888 | tf_op jit(solution)/shard_map/ppermute | solution.py:501
  13.6 1.3 %copy-start.1 = (s32[2,5,16,2048]{3,2,1,0:T(8,128)S(1)}, s32[2,5,16,2048]{3,2,1,0:T(8,128)}, u32[]{:S(2)}) copy-start(s32[2,5,16,2048]{3,2,1,0:T(8,128)} %thr_ref.3) | copy-start | bytes 3932164
  14.9 9.8 %copy-start.2 = (f32[2048]{0:T(1024)S(1)}, f32[2048]{0:T(1024)}, u32[]{:S(2)}) copy-start(f32[2048]{0:T(1024)} %param.9) | copy-start | bytes 24580
  14.9 9.8 %copy-start.3 = (f32[2048]{0:T(1024)S(1)}, f32[2048]{0:T(1024)}, u32[]{:S(2)}) copy-start(f32[2048]{0:T(1024)} %param.10) | copy-start | bytes 24580
  22.6 8.2 %copy-start.6 = (s32[5]{0:T(128)S(1)}, s32[5]{0:T(128)}, u32[]{:S(2)}) copy-start(s32[5]{0:T(128)} %partner_ref.1) | copy-start | bytes 64
  22.6 8.1 %copy-start.7 = (s32[5]{0:T(128)S(1)}, s32[5]{0:T(128)}, u32[]{:S(2)}) copy-start(s32[5]{0:T(128)} %accept_ref.1) | copy-start | bytes 64
  22.6 6.7 %collective-permute-start.5 = (f32[424,128]{1,0:T(8,128)S(1)}, f32[424,128]{1,0:T(8,128)S(1)}, u32[]{:S(2)}, u32[]{:S(2)}) collective-permute-start(f32[424,128]{1,0:T(8,128)S(1)} %get-tuple-element.28), channel_id=1, source_target_pairs={{0,2},{2,4},{4,6},{6,0},{1,3},{3,5},{5,7},{7,1},{8,10},{10,12},{12... | collective-permute-start | bytes 651272 | tf_op jit(solution)/shard_map/ppermute | solution.py:556
  23.2 7.6 %collective-permute-start.6 = (f32[424,128]{1,0:T(8,128)S(1)}, f32[424,128]{1,0:T(8,128)S(1)}, u32[]{:S(2)}, u32[]{:S(2)}) collective-permute-start(f32[424,128]{1,0:T(8,128)S(1)} %get-tuple-element.29), channel_id=1, source_target_pairs={{2,0},{4,2},{6,4},{0,6},{3,1},{5,3},{7,5},{1,7},{10,8},{12,10},{14... | collective-permute-start | bytes 651272 | tf_op jit(solution)/shard_map/ppermute | solution.py:557
  33.5 5.2 %collective-permute-start.7 = (f32[8,128]{1,0:T(8,128)S(1)}, f32[8,128]{1,0:T(8,128)S(1)}, u32[]{:S(2)}, u32[]{:S(2)}) collective-permute-start(f32[8,128]{1,0:T(8,128)S(1)} %get-tuple-element.31), channel_id=1, source_target_pairs={{0,1},{1,0},{2,3},{3,2},{4,5},{5,4},{6,7},{7,6},{8,9},{9,8},{10,11... | collective-permute-start | bytes 12296 | tf_op jit(solution)/shard_map/ppermute | solution.py:582

commit v3 on v2

--- a/solution.py
+++ b/solution.py
@@ -10,6 +10,7 @@
 CORE = TILES * PLANES
 CORE_MSG = CORE + 2
 EDGE = 10
+FAR_EDGE = EDGE + 1
 ROWQ = 10
 MESSAGE_ROWS = 424
 CHUNK = 5
@@ -143,6 +144,7 @@
             lambda side, half: edge_thr[side, config, half * 8 : half * 8 + 8],
             masks, out, base,
         )
+    far_edge_ref[EDGE] = jnp.zeros((8, 128), F32)
     for copy in small:
         copy.wait()
     for n, (config, out) in enumerate(((far, far_ref), (near, near_ref))):
@@ -157,25 +159,40 @@
         pack_config(*config_reader(spin_buf.at[n], thr_buf.at[n]), masks, put)
 
 
+class Either:
+    def __init__(self, first, ref, other):
+        self.first, self.ref, self.other = first, ref, other
+
+    def __getitem__(self, at):
+        return jnp.where(self.first, self.ref[at], self.other[at])
+
+
+def has_far():
+    rep = lax.axis_index("rep")
+    return jnp.logical_and(rep != 0, rep != lax.axis_size("rep") - 1)
+
+
 def inner_kernel(
     spins_ref, thr_ref, beta_ref, coup_ref,
     inner_ref, rows_ref, scale_ref,
     spin_buf, thr_buf, beta_buf, coup_buf, sem,
 ):
+    far = jnp.where(lax.rem(lax.axis_index("rep"), 2) == 0, 0, 4)
     copies = [
-        fetch(spins_ref, thr_ref, n + 1, spin_buf.at[n], thr_buf.at[n], sem, 3 * n) for n in range(3)
+        fetch(spins_ref, thr_ref, config, spin_buf.at[n], thr_buf.at[n], sem, 3 * n)
+        for n, config in enumerate((1, 2, 3, far))
     ]
-    small = scalars(beta_ref, coup_ref, beta_buf, coup_buf, sem, 9)
+    small = scalars(beta_ref, coup_ref, beta_buf, coup_buf, sem, 12)
     masks = (checker(), 7 - subs())
-    for n in range(3):
+    for n in range(4):
         for copy in copies[n]:
             copy.wait()
 
         def put(plane, k, value):
             inner_ref[n, k * PLANES + plane] = value
-            if plane < 7:
+            if n < 3 and plane < 7:
                 rows_ref[plane * TILES + k, n : n + 1] = value[0:1]
-            if 3 <= plane < 6:
+            if n < 3 and 3 <= plane < 6:
                 rows_ref[(plane + 4) * TILES + k, n : n + 1] = value[1:2]
 
         pack_config(*config_reader(spin_buf.at[n], thr_buf.at[n]), masks, put)
@@ -184,10 +201,11 @@
     sub = subs()
     for base, buf in ((0, beta_buf), (1, coup_buf)):
         scale_ref[base] = jnp.where(sub == 0, buf[1], jnp.where(sub == 1, buf[2], buf[3]))
+        scale_ref[2 + base] = jnp.full((8, 128), buf[far], F32)
 
 
 def slices_kernel(
-    rows_ref, scale_ref, x_ref, y_ref, inner_edge_ref, x_edge_ref, y_edge_ref,
+    rows_ref, scale_ref, inner_ref, x_ref, y_ref, inner_edge_ref, x_edge_ref, y_edge_ref,
     up_ref, down_ref, own_ref,
 ):
     sub = subs()
@@ -195,13 +213,16 @@
     low = lanes() < 64
     swap = jnp.bitwise_xor(lanes(), 1)
 
+    came = has_far()
+
     def five(mine, x, y):
         return jnp.where(sub == 3, x, jnp.where(sub == 4, y, mine))
 
     def row(q, k):
         plane, s = (q, 0) if q < 7 else (q - 4, 1)
         at = k * PLANES + plane
-        return five(rows_ref[q * TILES + k], x_ref[at, s : s + 1], y_ref[at, s : s + 1])
+        y = jnp.where(came, y_ref[at, s : s + 1], inner_ref[3, at, s : s + 1])
+        return five(rows_ref[q * TILES + k], x_ref[at, s : s + 1], y)
 
     for k in range(TILES):
         p0 = [row(c, k) for c in range(3)]
@@ -233,7 +254,8 @@
     down_ref[at:MESSAGE_ROWS] = jnp.zeros((MESSAGE_ROWS - at, 128), F32)
     up_ref[at:MESSAGE_ROWS] = jnp.zeros((MESSAGE_ROWS - at, 128), F32)
     for base in range(2):
-        own_ref[3 * TILES + base] = five(scale_ref[base], x_ref[CORE + base], y_ref[CORE + base])
+        y = jnp.where(came, y_ref[CORE + base], scale_ref[2 + base])
+        own_ref[3 * TILES + base] = five(scale_ref[base], x_ref[CORE + base], y)
 
 
 def row_neighbours():
@@ -255,7 +277,7 @@
 
 
 def core_list(inner_ref, x_ref, y_ref):
-    return [inner_ref.at[0], inner_ref.at[1], inner_ref.at[2], x_ref, y_ref]
+    return [inner_ref.at[0], inner_ref.at[1], inner_ref.at[2], x_ref, Either(has_far(), y_ref, inner_ref.at[3])]
 
 
 def space_field(bonds, at, above, here, turned, below, masks):
@@ -504,7 +526,7 @@
         front_kernel,
         out_shape=(
             shape(CORE_MSG, 8, 128), shape(CORE_MSG, 8, 128),
-            shape(EDGE, 8, 128), shape(EDGE, 8, 128), shape(3 * EDGE + 1, 8, 128),
+            shape(FAR_EDGE, 8, 128), shape(EDGE, 8, 128), shape(3 * EDGE + 1, 8, 128),
         ),
         in_specs=[hbm()] * 6,
         out_specs=(vmem(),) * 5,
@@ -522,7 +544,7 @@
         compiler_params=params(FRONT_LIMIT),
         name="front",
     )(spins, thresholds, betas, time_coupling, right, down)
-    far_core = lax.ppermute(far_core, "rep", [(r, far_of(r)) for r in range(ranks)])
+    far_core = lax.ppermute(far_core, "rep", [(r, far_of(r)) for r in range(ranks) if far_of(r) != r])
     inner_edge = lax.ppermute(inner_edge, "space", [(0, 1), (1, 0)])
     far_edge = crosswise(far_edge, far_of)
     near_edge = crosswise(near_edge, near_of)
@@ -530,15 +552,15 @@
 
     inner, rows, scale = pl.pallas_call(
         inner_kernel,
-        out_shape=(shape(3, CORE, 8, 128), shape(ROWQ * TILES, 8, 128), shape(2, 8, 128)),
+        out_shape=(shape(4, CORE, 8, 128), shape(ROWQ * TILES, 8, 128), shape(4, 8, 128)),
         in_specs=[hbm()] * 4,
         out_specs=(vmem(),) * 3,
         scratch_shapes=[
-            pltpu.VMEM((3, 3, 16, 2048), F32),
-            pltpu.VMEM((3, 2, 16, 2048), jnp.int32),
+            pltpu.VMEM((4, 3, 16, 2048), F32),
+            pltpu.VMEM((4, 2, 16, 2048), jnp.int32),
             pltpu.SMEM((5,), F32),
             pltpu.SMEM((5,), F32),
-            pltpu.SemaphoreType.DMA((11,)),
+            pltpu.SemaphoreType.DMA((14,)),
         ],
         compiler_params=params(INNER_LIMIT),
         name="pack_inner",
@@ -548,11 +570,11 @@
     up, down_msg, own = pl.pallas_call(
         slices_kernel,
         out_shape=(message, message, shape(3 * TILES + 2, 8, 128)),
-        in_specs=[vmem()] * 7,
+        in_specs=[vmem()] * 8,
         out_specs=(vmem(),) * 3,
         compiler_params=params(),
         name="slices",
-    )(rows, scale, near_core, far_core, inner_edge, near_edge, far_edge)
+    )(rows, scale, inner, near_core, far_core, inner_edge, near_edge, far_edge)
     from_before = lax.ppermute(up, "tm", [(t, (t + 1) % depth) for t in range(depth)])
     from_after = lax.ppermute(down_msg, "tm", [((t + 1) % depth, t) for t in range(depth)])
 

time: 39.4 us -> 38.4 us (0.975)
  the two profiles are of different devices: /device:TPU:6 before, /device:TPU:14 now
where the time goes in v3:
time: 38.4 us; the launch traced here: 38.2 us
  starting transfers between devices  13.8 us (36%)
  Pallas kernels  11.4 us (30%)
  waiting for transfers between devices  10.3 us (27%)
  local copies, waits for them, and re-layouts  1.35 us (4%)
  between operations  0.77 us (2%)
  other arithmetic  0.6 us (2%)
    ppermute x1, starting transfers between devices, on_device(): lax.ppermute(far_core, 'rep', [(r, far_of(r)) for r in range(ranks) if fa...  7.74 us
    ppermute x1, waiting for transfers between devices, on_device(): lax.ppermute(up, 'tm', [(t, (t + 1) % depth) for t in range(depth)])  3.8 us
    pallas_call x1, Pallas kernels, on_device(): pl.pallas_call(sweep_kernel, out_shape=(shape(5, TILES * 6, 8, 128), shap...  2.83 us
    pallas_call x1, Pallas kernels, on_device(): pl.pallas_call(inner_kernel, out_shape=(shape(4, CORE, 8, 128), shape(ROW...  2.77 us
    pallas_call x1, Pallas kernels, on_device(): pl.pallas_call(front_kernel, out_shape=(shape(CORE_MSG, 8, 128), shape(CO...  2.77 us
    ppermute x1, starting transfers between devices, on_device(): inner_edge = lax.ppermute(inner_edge, 'space', [(0, 1), (1, 0)])  2.68 us
    ppermute x1, waiting for transfers between devices, on_device(): other_energy = lax.ppermute(energy, 'space', [(0, 1), (1, 0)])  2.63 us
    ppermute x2, waiting for transfers between devices, crosswise(): return lax.ppermute(x, axes, pairs)  2.47 us
  transfers between devices with their start and end apart: 8, of which 5 were waited for; matrix products, arithmetic and copies ran while one was open for 0% of the time, Pallas kernels for 15%

profile of v3, /device:TPU:14, one launch (start us, length us, event | category | flops | bytes accessed | tf_op | source)
XLA Modules:
  0.0 38.2 jit_solution(10374223060251432965)
XLA Ops:
  0.7 2.8 %front.1 = (f32[130,8,128]{2,1,0:T(8,128)}, f32[130,8,128]{2,1,0:T(8,128)}, f32[11,8,128]{2,1,0:T(8,128)}, f32[10,8,128]{2,1,0:T(8,128)}, f32[31,8,128]{2,1,0:T(8,128)}) custom-call(f32[5,3,16,2048]{3,2,1,0:T(8,128)} %spins_ref.3, s32[2,5,16,2048]{3,2,1,0:T(8,128)} %thr_ref.3, f32[5]{0:T(128)} %beta_ref.3, f32[5]{0:T(128)} %coup_ref.3, f32[16,128]{1,0:T(8,128)} %bitcast.3, ...), custom_call_target="tpu_custom_call" | custom-call | tf_op jit(solution)/shard_map/front/pallas_call | solution.py:525
  3.4 0.1 collective-permute-start
  3.5 7.7 %collective-permute-start.1 = (f32[130,8,128]{2,1,0:T(8,128)}, f32[130,8,128]{2,1,0:T(8,128)S(1)}, u32[]{:S(2)}, u32[]{:S(2)}) collective-permute-start(f32[130,8,128]{2,1,0:T(8,128)} %get-tuple-element.19), channel_id=1, source_target_pairs={{8,16},{16,8},{24,32},{32,24},{40,48},{48,40},{56,64},{64,56},{72,... | collective-permute-start | bytes 1597448 | tf_op jit(solution)/shard_map/ppermute | solution.py:547
  11.3 2.7 %collective-permute-start.2 = (f32[31,8,128]{2,1,0:T(8,128)}, f32[31,8,128]{2,1,0:T(8,128)S(1)}, u32[]{:S(2)}, u32[]{:S(2)}) collective-permute-start(f32[31,8,128]{2,1,0:T(8,128)} %get-tuple-element.20), channel_id=1, source_target_pairs={{0,1},{1,0},{2,3},{3,2},{4,5},{5,4},{6,7},{7,6},{8,9},{9,8},{10,11... | collective-permute-start | bytes 380936 | tf_op jit(solution)/shard_map/ppermute | solution.py:548
  14.0 0.0 collective-permute-start.4
  14.0 0.0 collective-permute-start.3
  14.0 0.0 copy-done.4
  14.0 0.0 copy-done
  14.0 0.0 copy-start.1
  14.0 1.3 %copy-done.1 = s32[2,5,16,2048]{3,2,1,0:T(8,128)S(1)} copy-done((s32[2,5,16,2048]{3,2,1,0:T(8,128)S(1)}, s32[2,5,16,2048]{3,2,1,0:T(8,128)}, u32[]{:S(2)}) %copy-start.1) | copy-done | bytes 1310744
  15.3 2.8 %pack_inner.1 = (f32[4,128,8,128]{3,2,1,0:T(8,128)S(1)}, f32[160,8,128]{2,1,0:T(8,128)S(1)}, f32[4,8,128]{2,1,0:T(8,128)S(1)}) custom-call(f32[5,3,16,2048]{3,2,1,0:T(8,128)S(1)} %copy-done, s32[2,5,16,2048]{3,2,1,0:T(8,128)S(1)} %copy-done.1, f32[5]{0:T(128)S(1)} %copy-done.4, f32[5]{0:T(128)S(1)} %copy-done.5), custom_call_target="tpu_custom_call" | custom-call | tf_op jit(solution)/shard_map/pack_inner/pallas_call | solution.py:553
  18.1 1.3 %collective-permute-done.3.x_edge_ref = f32[10,8,128]{2,1,0:T(8,128)S(1)} collective-permute-done((f32[10,8,128]{2,1,0:T(8,128)}, f32[10,8,128]{2,1,0:T(8,128)S(1)}, u32[]{:S(2)}, u32[]{:S(2)}) %collective-permute-start.3) | collective-permute-done | bytes 40992 | tf_op jit(solution)/shard_map/ppermute | solution.py:523
  19.4 1.2 %collective-permute-done.4.y_edge_ref = f32[11,8,128]{2,1,0:T(8,128)S(1)} collective-permute-done((f32[11,8,128]{2,1,0:T(8,128)}, f32[11,8,128]{2,1,0:T(8,128)S(1)}, u32[]{:S(2)}, u32[]{:S(2)}) %collective-permute-start.4) | collective-permute-done | bytes 45088 | tf_op jit(solution)/shard_map/ppermute | solution.py:523
  20.6 0.0 collective-permute-done.2.inner_edge_ref
  20.6 0.0 collective-permute-done.x_ref
  20.6 0.0 collective-permute-done.1.y_ref
  20.6 0.0 copy-start.2
  20.6 0.0 copy-start.3
  20.6 0.2 slices.1
  20.8 0.0 copy-start.6
  20.8 0.0 copy-start.7
  20.8 0.6 %collective-permute-start.5 = (f32[424,128]{1,0:T(8,128)S(1)}, f32[424,128]{1,0:T(8,128)S(1)}, u32[]{:S(2)}, u32[]{:S(2)}) collective-permute-start(f32[424,128]{1,0:T(8,128)S(1)} %get-tuple-element.28), channel_id=1, source_target_pairs={{0,2},{2,4},{4,6},{6,0},{1,3},{3,5},{5,7},{7,1},{8,10},{10,12},{12... | collective-permute-start | bytes 651272 | tf_op jit(solution)/shard_map/ppermute | solution.py:578
  21.4 1.5 %collective-permute-start.6 = (f32[424,128]{1,0:T(8,128)S(1)}, f32[424,128]{1,0:T(8,128)S(1)}, u32[]{:S(2)}, u32[]{:S(2)}) collective-permute-start(f32[424,128]{1,0:T(8,128)S(1)} %get-tuple-element.29), channel_id=1, source_target_pairs={{2,0},{4,2},{6,4},{0,6},{3,1},{5,3},{7,5},{1,7},{10,8},{12,10},{14... | collective-permute-start | bytes 651272 | tf_op jit(solution)/shard_map/ppermute | solution.py:579
  23.0 1.5 %prepare.1 = (f32[5,54,8,128]{3,2,1,0:T(8,128)S(1)}, f32[72,8,128]{2,1,0:T(8,128)S(1)}) custom-call(f32[4,128,8,128]{3,2,1,0:T(8,128)S(1)} %get-tuple-element.17.inner_ref, f32[130,8,128]{2,1,0:T(8,128)S(1)} %collective-permute-done.x_ref, f32[130,8,128]{2,1,0:T(8,128)S(1)} %collective-permute-done.1.y_ref, ...), custom_call_target="tpu_custom_call" | custom-call | tf_op jit(solution)/shard_map/prepare/pallas_call | solution.py:582
  24.4 3.8 %collective-permute-done.5.up_ref = f32[424,128]{1,0:T(8,128)S(1)} collective-permute-done((f32[424,128]{1,0:T(8,128)S(1)}, f32[424,128]{1,0:T(8,128)S(1)}, u32[]{:S(2)}, u32[]{:S(2)}) %collective-permute-start.5) | collective-permute-done | bytes 217120 | tf_op jit(solution)/shard_map/ppermute | solution.py:578
  28.2 1.4 %collective-permute-done.6.down_ref = f32[424,128]{1,0:T(8,128)S(1)} collective-permute-done((f32[424,128]{1,0:T(8,128)S(1)}, f32[424,128]{1,0:T(8,128)S(1)}, u32[]{:S(2)}, u32[]{:S(2)}) %collective-permute-start.6) | collective-permute-done | bytes 217120 | tf_op jit(solution)/shard_map/ppermute | solution.py:579
  29.6 0.0 copy-done.7
  29.6 2.8 %sweep.1 = (f32[5,96,8,128]{3,2,1,0:T(8,128)S(1)}, f32[8,128]{1,0:T(8,128)S(1)}) custom-call(f32[4,128,8,128]{3,2,1,0:T(8,128)S(1)} %get-tuple-element.17.inner_ref, f32[130,8,128]{2,1,0:T(8,128)S(1)} %collective-permute-done.x_ref, f32[130,8,128]{2,1,0:T(8,128)S(1)} %collective-permute-done.1.y_ref, ...), custom_call_target="tpu_custom_call" | custom-call | tf_op jit(solution)/shard_map/sweep/pallas_call | solution.py:590
  32.5 1.2 %collective-permute-start.7 = (f32[8,128]{1,0:T(8,128)S(1)}, f32[8,128]{1,0:T(8,128)S(1)}, u32[]{:S(2)}, u32[]{:S(2)}) collective-permute-start(f32[8,128]{1,0:T(8,128)S(1)} %get-tuple-element.31), channel_id=1, source_target_pairs={{0,1},{1,0},{2,3},{3,2},{4,5},{5,4},{6,7},{7,6},{8,9},{9,8},{10,11... | collective-permute-start | bytes 12296 | tf_op jit(solution)/shard_map/ppermute | solution.py:604
  33.6 1.3 %unpack.1 = f32[5,3,16,2048]{3,2,1,0:T(8,128)} custom-call(f32[5,96,8,128]{3,2,1,0:T(8,128)S(1)} %get-tuple-element.30.final_ref), custom_call_target="tpu_custom_call" | custom-call | tf_op jit(solution)/shard_map/unpack/pallas_call | solution.py:605
  35.0 2.6 %collective-permute-done.7 = f32[8,128]{1,0:T(8,128)S(1)} collective-permute-done((f32[8,128]{1,0:T(8,128)S(1)}, f32[8,128]{1,0:T(8,128)S(1)}, u32[]{:S(2)}, u32[]{:S(2)}) %collective-permute-start.7) | collective-permute-done | bytes 4128 | tf_op jit(solution)/shard_map/ppermute | solution.py:604
  37.6 0.6 %add.3 = f32[8,128]{1,0:T(8,128)} add(f32[8,128]{1,0:T(8,128)S(1)} %get-tuple-element.31, f32[8,128]{1,0:T(8,128)S(1)} %collective-permute-done.7) | non-fusion elementwise | flops 1024 | bytes 12288 | tf_op jit(solution)/shard_map/add | solution.py:614
  (7 shorter events, 0.0 us)
Async XLA Ops:
  0.6 13.3 %copy-start.5 = (f32[5]{0:T(128)S(1)}, f32[5]{0:T(128)}, u32[]{:S(2)}) copy-start(f32[5]{0:T(128)} %coup_ref.3) | copy-start | bytes 64
  0.6 13.3 %copy-start.4 = (f32[5]{0:T(128)S(1)}, f32[5]{0:T(128)}, u32[]{:S(2)}) copy-start(f32[5]{0:T(128)} %beta_ref.3) | copy-start | bytes 64
  0.6 13.3 %copy-start = (f32[5,3,16,2048]{3,2,1,0:T(8,128)S(1)}, f32[5,3,16,2048]{3,2,1,0:T(8,128)}, u32[]{:S(2)}) copy-start(f32[5,3,16,2048]{3,2,1,0:T(8,128)} %spins_ref.3) | copy-start | bytes 5898244
  3.4 17.1 %collective-permute-start = (f32[130,8,128]{2,1,0:T(8,128)}, f32[130,8,128]{2,1,0:T(8,128)S(1)}, u32[]{:S(2)}, u32[]{:S(2)}) collective-permute-start(f32[130,8,128]{2,1,0:T(8,128)} %get-tuple-element.18), channel_id=1, source_target_pairs={{0,8},{8,0},{16,24},{24,16},{32,40},{40,32},{48,56},{56,48},{64,72... | collective-permute-start | bytes 1597448 | tf_op jit(solution)/shard_map/ppermute | solution.py:551
  3.5 17.0 %collective-permute-start.1 = (f32[130,8,128]{2,1,0:T(8,128)}, f32[130,8,128]{2,1,0:T(8,128)S(1)}, u32[]{:S(2)}, u32[]{:S(2)}) collective-permute-start(f32[130,8,128]{2,1,0:T(8,128)} %get-tuple-element.19), channel_id=1, source_target_pairs={{8,16},{16,8},{24,32},{32,24},{40,48},{48,40},{56,64},{64,56},{72,... | collective-permute-start | bytes 1597448 | tf_op jit(solution)/shard_map/ppermute | solution.py:547
  11.3 9.3 %collective-permute-start.2 = (f32[31,8,128]{2,1,0:T(8,128)}, f32[31,8,128]{2,1,0:T(8,128)S(1)}, u32[]{:S(2)}, u32[]{:S(2)}) collective-permute-start(f32[31,8,128]{2,1,0:T(8,128)} %get-tuple-element.20), channel_id=1, source_target_pairs={{0,1},{1,0},{2,3},{3,2},{4,5},{5,4},{6,7},{7,6},{8,9},{9,8},{10,11... | collective-permute-start | bytes 380936 | tf_op jit(solution)/shard_map/ppermute | solution.py:548
  14.0 6.6 %collective-permute-start.4 = (f32[11,8,128]{2,1,0:T(8,128)}, f32[11,8,128]{2,1,0:T(8,128)S(1)}, u32[]{:S(2)}, u32[]{:S(2)}) collective-permute-start(f32[11,8,128]{2,1,0:T(8,128)} %get-tuple-element.22), channel_id=1, source_target_pairs={{0,1},{1,0},{2,3},{3,2},{4,5},{5,4},{6,7},{7,6},{8,17},{9,16},{10,... | collective-permute-start | bytes 135176 | tf_op jit(solution)/shard_map/ppermute | solution.py:523
  14.0 5.4 %collective-permute-start.3 = (f32[10,8,128]{2,1,0:T(8,128)}, f32[10,8,128]{2,1,0:T(8,128)S(1)}, u32[]{:S(2)}, u32[]{:S(2)}) collective-permute-start(f32[10,8,128]{2,1,0:T(8,128)} %get-tuple-element.21), channel_id=1, source_target_pairs={{0,9},{1,8},{2,11},{3,10},{4,13},{5,12},{6,15},{7,14},{8,1},{9,0},... | collective-permute-start | bytes 122888 | tf_op jit(solution)/shard_map/ppermute | solution.py:523
  14.0 1.3 %copy-start.1 = (s32[2,5,16,2048]{3,2,1,0:T(8,128)S(1)}, s32[2,5,16,2048]{3,2,1,0:T(8,128)}, u32[]{:S(2)}) copy-start(s32[2,5,16,2048]{3,2,1,0:T(8,128)} %thr_ref.3) | copy-start | bytes 3932164
  20.6 2.4 %copy-start.2 = (f32[2048]{0:T(1024)S(1)}, f32[2048]{0:T(1024)}, u32[]{:S(2)}) copy-start(f32[2048]{0:T(1024)} %param.9) | copy-start | bytes 24580
  20.6 2.4 %copy-start.3 = (f32[2048]{0:T(1024)S(1)}, f32[2048]{0:T(1024)}, u32[]{:S(2)}) copy-start(f32[2048]{0:T(1024)} %param.10) | copy-start | bytes 24580
  20.8 8.8 %copy-start.6 = (s32[5]{0:T(128)S(1)}, s32[5]{0:T(128)}, u32[]{:S(2)}) copy-start(s32[5]{0:T(128)} %partner_ref.1) | copy-start | bytes 64
  20.8 8.8 %copy-start.7 = (s32[5]{0:T(128)S(1)}, s32[5]{0:T(128)}, u32[]{:S(2)}) copy-start(s32[5]{0:T(128)} %accept_ref.1) | copy-start | bytes 64
  20.8 7.4 %collective-permute-start.5 = (f32[424,128]{1,0:T(8,128)S(1)}, f32[424,128]{1,0:T(8,128)S(1)}, u32[]{:S(2)}, u32[]{:S(2)}) collective-permute-start(f32[424,128]{1,0:T(8,128)S(1)} %get-tuple-element.28), channel_id=1, source_target_pairs={{0,2},{2,4},{4,6},{6,0},{1,3},{3,5},{5,7},{7,1},{8,10},{10,12},{12... | collective-permute-start | bytes 651272 | tf_op jit(solution)/shard_map/ppermute | solution.py:578
  21.4 8.2 %collective-permute-start.6 = (f32[424,128]{1,0:T(8,128)S(1)}, f32[424,128]{1,0:T(8,128)S(1)}, u32[]{:S(2)}, u32[]{:S(2)}) collective-permute-start(f32[424,128]{1,0:T(8,128)S(1)} %get-tuple-element.29), channel_id=1, source_target_pairs={{2,0},{4,2},{6,4},{0,6},{3,1},{5,3},{7,5},{1,7},{10,8},{12,10},{14... | collective-permute-start | bytes 651272 | tf_op jit(solution)/shard_map/ppermute | solution.py:579
  32.5 5.2 %collective-permute-start.7 = (f32[8,128]{1,0:T(8,128)S(1)}, f32[8,128]{1,0:T(8,128)S(1)}, u32[]{:S(2)}, u32[]{:S(2)}) collective-permute-start(f32[8,128]{1,0:T(8,128)S(1)} %get-tuple-element.31), channel_id=1, source_target_pairs={{0,1},{1,0},{2,3},{3,2},{4,5},{5,4},{6,7},{7,6},{8,9},{9,8},{10,11... | collective-permute-start | bytes 12296 | tf_op jit(solution)/shard_map/ppermute | solution.py:604

commit v4 on v3

--- a/solution.py
+++ b/solution.py
@@ -180,19 +180,19 @@
     far = jnp.where(lax.rem(lax.axis_index("rep"), 2) == 0, 0, 4)
     copies = [
         fetch(spins_ref, thr_ref, config, spin_buf.at[n], thr_buf.at[n], sem, 3 * n)
-        for n, config in enumerate((1, 2, 3, far))
+        for n, config in enumerate((1, 2, 3))
     ]
     small = scalars(beta_ref, coup_ref, beta_buf, coup_buf, sem, 12)
     masks = (checker(), 7 - subs())
-    for n in range(4):
+    for n in range(3):
         for copy in copies[n]:
             copy.wait()
 
         def put(plane, k, value):
             inner_ref[n, k * PLANES + plane] = value
-            if n < 3 and plane < 7:
+            if plane < 7:
                 rows_ref[plane * TILES + k, n : n + 1] = value[0:1]
-            if n < 3 and 3 <= plane < 6:
+            if 3 <= plane < 6:
                 rows_ref[(plane + 4) * TILES + k, n : n + 1] = value[1:2]
 
         pack_config(*config_reader(spin_buf.at[n], thr_buf.at[n]), masks, put)
@@ -202,6 +202,16 @@
     for base, buf in ((0, beta_buf), (1, coup_buf)):
         scale_ref[base] = jnp.where(sub == 0, buf[1], jnp.where(sub == 1, buf[2], buf[3]))
         scale_ref[2 + base] = jnp.full((8, 128), buf[far], F32)
+
+    @pl.when(jnp.logical_not(has_far()))
+    def _():
+        for copy in fetch(spins_ref, thr_ref, far, spin_buf.at[3], thr_buf.at[3], sem, 9):
+            copy.wait()
+
+        def put_far(plane, k, value):
+            inner_ref[3, k * PLANES + plane] = value
+
+        pack_config(*config_reader(spin_buf.at[3], thr_buf.at[3]), masks, put_far)
 
 
 def slices_kernel(

time: 38.4 us -> 37.9 us (0.987)
  the two profiles are of different devices: /device:TPU:14 before, /device:TPU:6 now
where the time goes in v4:
time: 37.9 us; the launch traced here: 37.2 us
  starting transfers between devices  16.5 us (44%)
  Pallas kernels  11.5 us (30%)
  waiting for transfers between devices  6.51 us (17%)
  local copies, waits for them, and re-layouts  1.35 us (4%)
  between operations  0.76 us (2%)
  other arithmetic  0.6 us (2%)
    ppermute x2, starting transfers between devices, crosswise(): return lax.ppermute(x, axes, pairs)  6.02 us
    ppermute x1, starting transfers between devices, on_device(): other_energy = lax.ppermute(energy, 'space', [(0, 1), (1, 0)])  4.36 us
    ppermute x1, starting transfers between devices, on_device(): inner_edge = lax.ppermute(inner_edge, 'space', [(0, 1), (1, 0)])  3.28 us
    ppermute x1, waiting for transfers between devices, on_device(): lax.ppermute(up, 'tm', [(t, (t + 1) % depth) for t in range(depth)])  2.84 us
    pallas_call x1, Pallas kernels, on_device(): pl.pallas_call(sweep_kernel, out_shape=(shape(5, TILES * 6, 8, 128), shap...  2.83 us
    pallas_call x1, Pallas kernels, on_device(): pl.pallas_call(inner_kernel, out_shape=(shape(4, CORE, 8, 128), shape(ROW...  2.83 us
    pallas_call x1, Pallas kernels, on_device(): pl.pallas_call(front_kernel, out_shape=(shape(CORE_MSG, 8, 128), shape(CO...  2.77 us
    ppermute x1, waiting for transfers between devices, on_device(): lax.ppermute(down_msg, 'tm', [((t + 1) % depth, t) for t in range(depth)])  1.97 us
  transfers between devices with their start and end apart: 8, of which 4 were waited for; matrix products, arithmetic and copies ran while one was open for 0% of the time, Pallas kernels for 15%

profile of v4, /device:TPU:6, one launch (start us, length us, event | category | flops | bytes accessed | tf_op | source)
XLA Modules:
  0.0 37.2 jit_solution(1167328812834344162)
XLA Ops:
  0.6 0.0 copy-start.5
  0.6 0.0 copy-start.4
  0.6 0.0 copy-start
  0.7 2.8 %front.1 = (f32[130,8,128]{2,1,0:T(8,128)}, f32[130,8,128]{2,1,0:T(8,128)}, f32[11,8,128]{2,1,0:T(8,128)}, f32[10,8,128]{2,1,0:T(8,128)}, f32[31,8,128]{2,1,0:T(8,128)}) custom-call(f32[5,3,16,2048]{3,2,1,0:T(8,128)} %spins_ref.3, s32[2,5,16,2048]{3,2,1,0:T(8,128)} %thr_ref.3, f32[5]{0:T(128)} %beta_ref.3, f32[5]{0:T(128)} %coup_ref.3, f32[16,128]{1,0:T(8,128)} %bitcast.3, ...), custom_call_target="tpu_custom_call" | custom-call | tf_op jit(solution)/shard_map/front/pallas_call | solution.py:535
  3.4 0.1 collective-permute-start
  3.5 0.7 %collective-permute-start.1 = (f32[130,8,128]{2,1,0:T(8,128)}, f32[130,8,128]{2,1,0:T(8,128)S(1)}, u32[]{:S(2)}, u32[]{:S(2)}) collective-permute-start(f32[130,8,128]{2,1,0:T(8,128)} %get-tuple-element.19), channel_id=1, source_target_pairs={{8,16},{16,8},{24,32},{32,24},{40,48},{48,40},{56,64},{64,56},{72,... | collective-permute-start | bytes 1597448 | tf_op jit(solution)/shard_map/ppermute | solution.py:557
  4.2 3.3 %collective-permute-start.2 = (f32[31,8,128]{2,1,0:T(8,128)}, f32[31,8,128]{2,1,0:T(8,128)S(1)}, u32[]{:S(2)}, u32[]{:S(2)}) collective-permute-start(f32[31,8,128]{2,1,0:T(8,128)} %get-tuple-element.20), channel_id=1, source_target_pairs={{0,1},{1,0},{2,3},{3,2},{4,5},{5,4},{6,7},{7,6},{8,9},{9,8},{10,11... | collective-permute-start | bytes 380936 | tf_op jit(solution)/shard_map/ppermute | solution.py:558
  7.5 0.3 collective-permute-start.4
  7.9 5.7 %collective-permute-start.3 = (f32[10,8,128]{2,1,0:T(8,128)}, f32[10,8,128]{2,1,0:T(8,128)S(1)}, u32[]{:S(2)}, u32[]{:S(2)}) collective-permute-start(f32[10,8,128]{2,1,0:T(8,128)} %get-tuple-element.21), channel_id=1, source_target_pairs={{0,9},{1,8},{2,11},{3,10},{4,13},{5,12},{6,15},{7,14},{8,1},{9,0},... | collective-permute-start | bytes 122888 | tf_op jit(solution)/shard_map/ppermute | solution.py:533
  13.5 0.0 copy-done.4
  13.6 1.3 %copy-done.1 = s32[2,5,16,2048]{3,2,1,0:T(8,128)S(1)} copy-done((s32[2,5,16,2048]{3,2,1,0:T(8,128)S(1)}, s32[2,5,16,2048]{3,2,1,0:T(8,128)}, u32[]{:S(2)}) %copy-start.1) | copy-done | bytes 1310744
  14.9 2.8 %pack_inner.1 = (f32[4,128,8,128]{3,2,1,0:T(8,128)S(1)}, f32[160,8,128]{2,1,0:T(8,128)S(1)}, f32[4,8,128]{2,1,0:T(8,128)S(1)}) custom-call(f32[5,3,16,2048]{3,2,1,0:T(8,128)S(1)} %copy-done, s32[2,5,16,2048]{3,2,1,0:T(8,128)S(1)} %copy-done.1, f32[5]{0:T(128)S(1)} %copy-done.4, f32[5]{0:T(128)S(1)} %copy-done.5), custom_call_target="tpu_custom_call" | custom-call | tf_op jit(solution)/shard_map/pack_inner/pallas_call | solution.py:563
  17.7 1.5 %collective-permute-done.3.x_edge_ref = f32[10,8,128]{2,1,0:T(8,128)S(1)} collective-permute-done((f32[10,8,128]{2,1,0:T(8,128)}, f32[10,8,128]{2,1,0:T(8,128)S(1)}, u32[]{:S(2)}, u32[]{:S(2)}) %collective-permute-start.3) | collective-permute-done | bytes 40992 | tf_op jit(solution)/shard_map/ppermute | solution.py:533
  19.2 0.0 collective-permute-done.4.y_edge_ref
  19.2 0.0 collective-permute-done.2.inner_edge_ref
  19.2 0.0 collective-permute-done.x_ref
  19.2 0.0 collective-permute-done.1.y_ref
  19.2 0.0 copy-start.2
  19.2 0.0 copy-start.3
  19.2 0.2 slices.1
  19.4 0.0 copy-start.6
  19.4 0.0 copy-start.7
  19.4 0.6 %collective-permute-start.5 = (f32[424,128]{1,0:T(8,128)S(1)}, f32[424,128]{1,0:T(8,128)S(1)}, u32[]{:S(2)}, u32[]{:S(2)}) collective-permute-start(f32[424,128]{1,0:T(8,128)S(1)} %get-tuple-element.28), channel_id=1, source_target_pairs={{0,2},{2,4},{4,6},{6,0},{1,3},{3,5},{5,7},{7,1},{8,10},{10,12},{12... | collective-permute-start | bytes 651272 | tf_op jit(solution)/shard_map/ppermute | solution.py:588
  20.0 1.5 %collective-permute-start.6 = (f32[424,128]{1,0:T(8,128)S(1)}, f32[424,128]{1,0:T(8,128)S(1)}, u32[]{:S(2)}, u32[]{:S(2)}) collective-permute-start(f32[424,128]{1,0:T(8,128)S(1)} %get-tuple-element.29), channel_id=1, source_target_pairs={{2,0},{4,2},{6,4},{0,6},{3,1},{5,3},{7,5},{1,7},{10,8},{12,10},{14... | collective-permute-start | bytes 651272 | tf_op jit(solution)/shard_map/ppermute | solution.py:589
  21.6 1.5 %prepare.1 = (f32[5,54,8,128]{3,2,1,0:T(8,128)S(1)}, f32[72,8,128]{2,1,0:T(8,128)S(1)}) custom-call(f32[4,128,8,128]{3,2,1,0:T(8,128)S(1)} %get-tuple-element.17.inner_ref, f32[130,8,128]{2,1,0:T(8,128)S(1)} %collective-permute-done.x_ref, f32[130,8,128]{2,1,0:T(8,128)S(1)} %collective-permute-done.1.y_ref, ...), custom_call_target="tpu_custom_call" | custom-call | tf_op jit(solution)/shard_map/prepare/pallas_call | solution.py:592
  23.0 2.8 %collective-permute-done.5.up_ref = f32[424,128]{1,0:T(8,128)S(1)} collective-permute-done((f32[424,128]{1,0:T(8,128)S(1)}, f32[424,128]{1,0:T(8,128)S(1)}, u32[]{:S(2)}, u32[]{:S(2)}) %collective-permute-start.5) | collective-permute-done | bytes 217120 | tf_op jit(solution)/shard_map/ppermute | solution.py:588
  25.9 2.0 %collective-permute-done.6.down_ref = f32[424,128]{1,0:T(8,128)S(1)} collective-permute-done((f32[424,128]{1,0:T(8,128)S(1)}, f32[424,128]{1,0:T(8,128)S(1)}, u32[]{:S(2)}, u32[]{:S(2)}) %collective-permute-start.6) | collective-permute-done | bytes 217120 | tf_op jit(solution)/shard_map/ppermute | solution.py:589
  27.8 2.8 %sweep.1 = (f32[5,96,8,128]{3,2,1,0:T(8,128)S(1)}, f32[8,128]{1,0:T(8,128)S(1)}) custom-call(f32[4,128,8,128]{3,2,1,0:T(8,128)S(1)} %get-tuple-element.17.inner_ref, f32[130,8,128]{2,1,0:T(8,128)S(1)} %collective-permute-done.x_ref, f32[130,8,128]{2,1,0:T(8,128)S(1)} %collective-permute-done.1.y_ref, ...), custom_call_target="tpu_custom_call" | custom-call | tf_op jit(solution)/shard_map/sweep/pallas_call | solution.py:600
  30.7 4.4 %collective-permute-start.7 = (f32[8,128]{1,0:T(8,128)S(1)}, f32[8,128]{1,0:T(8,128)S(1)}, u32[]{:S(2)}, u32[]{:S(2)}) collective-permute-start(f32[8,128]{1,0:T(8,128)S(1)} %get-tuple-element.31), channel_id=1, source_target_pairs={{0,1},{1,0},{2,3},{3,2},{4,5},{5,4},{6,7},{7,6},{8,9},{9,8},{10,11... | collective-permute-start | bytes 12296 | tf_op jit(solution)/shard_map/ppermute | solution.py:614
  35.0 1.3 %unpack.1 = f32[5,3,16,2048]{3,2,1,0:T(8,128)} custom-call(f32[5,96,8,128]{3,2,1,0:T(8,128)S(1)} %get-tuple-element.30.final_ref), custom_call_target="tpu_custom_call" | custom-call | tf_op jit(solution)/shard_map/unpack/pallas_call | solution.py:615
  36.4 0.2 collective-permute-done.7
  36.6 0.6 %add.3 = f32[8,128]{1,0:T(8,128)} add(f32[8,128]{1,0:T(8,128)S(1)} %get-tuple-element.31, f32[8,128]{1,0:T(8,128)S(1)} %collective-permute-done.7) | non-fusion elementwise | flops 1024 | bytes 12288 | tf_op jit(solution)/shard_map/add | solution.py:624
  (7 shorter events, 0.0 us)
Async XLA Ops:
  0.6 12.9 %copy-start.5 = (f32[5]{0:T(128)S(1)}, f32[5]{0:T(128)}, u32[]{:S(2)}) copy-start(f32[5]{0:T(128)} %coup_ref.3) | copy-start | bytes 64
  0.6 12.9 %copy-start.4 = (f32[5]{0:T(128)S(1)}, f32[5]{0:T(128)}, u32[]{:S(2)}) copy-start(f32[5]{0:T(128)} %beta_ref.3) | copy-start | bytes 64
  0.6 12.9 %copy-start = (f32[5,3,16,2048]{3,2,1,0:T(8,128)S(1)}, f32[5,3,16,2048]{3,2,1,0:T(8,128)}, u32[]{:S(2)}) copy-start(f32[5,3,16,2048]{3,2,1,0:T(8,128)} %spins_ref.3) | copy-start | bytes 5898244
  3.4 15.7 %collective-permute-start = (f32[130,8,128]{2,1,0:T(8,128)}, f32[130,8,128]{2,1,0:T(8,128)S(1)}, u32[]{:S(2)}, u32[]{:S(2)}) collective-permute-start(f32[130,8,128]{2,1,0:T(8,128)} %get-tuple-element.18), channel_id=1, source_target_pairs={{0,8},{8,0},{16,24},{24,16},{32,40},{40,32},{48,56},{56,48},{64,72... | collective-permute-start | bytes 1597448 | tf_op jit(solution)/shard_map/ppermute | solution.py:561
  3.5 15.6 %collective-permute-start.1 = (f32[130,8,128]{2,1,0:T(8,128)}, f32[130,8,128]{2,1,0:T(8,128)S(1)}, u32[]{:S(2)}, u32[]{:S(2)}) collective-permute-start(f32[130,8,128]{2,1,0:T(8,128)} %get-tuple-element.19), channel_id=1, source_target_pairs={{8,16},{16,8},{24,32},{32,24},{40,48},{48,40},{56,64},{64,56},{72,... | collective-permute-start | bytes 1597448 | tf_op jit(solution)/shard_map/ppermute | solution.py:557
  4.2 14.9 %collective-permute-start.2 = (f32[31,8,128]{2,1,0:T(8,128)}, f32[31,8,128]{2,1,0:T(8,128)S(1)}, u32[]{:S(2)}, u32[]{:S(2)}) collective-permute-start(f32[31,8,128]{2,1,0:T(8,128)} %get-tuple-element.20), channel_id=1, source_target_pairs={{0,1},{1,0},{2,3},{3,2},{4,5},{5,4},{6,7},{7,6},{8,9},{9,8},{10,11... | collective-permute-start | bytes 380936 | tf_op jit(solution)/shard_map/ppermute | solution.py:558
  7.5 11.6 %collective-permute-start.4 = (f32[11,8,128]{2,1,0:T(8,128)}, f32[11,8,128]{2,1,0:T(8,128)S(1)}, u32[]{:S(2)}, u32[]{:S(2)}) collective-permute-start(f32[11,8,128]{2,1,0:T(8,128)} %get-tuple-element.22), channel_id=1, source_target_pairs={{0,1},{1,0},{2,3},{3,2},{4,5},{5,4},{6,7},{7,6},{8,17},{9,16},{10,... | collective-permute-start | bytes 135176 | tf_op jit(solution)/shard_map/ppermute | solution.py:533
  7.9 11.3 %collective-permute-start.3 = (f32[10,8,128]{2,1,0:T(8,128)}, f32[10,8,128]{2,1,0:T(8,128)S(1)}, u32[]{:S(2)}, u32[]{:S(2)}) collective-permute-start(f32[10,8,128]{2,1,0:T(8,128)} %get-tuple-element.21), channel_id=1, source_target_pairs={{0,9},{1,8},{2,11},{3,10},{4,13},{5,12},{6,15},{7,14},{8,1},{9,0},... | collective-permute-start | bytes 122888 | tf_op jit(solution)/shard_map/ppermute | solution.py:533
  13.5 1.3 %copy-start.1 = (s32[2,5,16,2048]{3,2,1,0:T(8,128)S(1)}, s32[2,5,16,2048]{3,2,1,0:T(8,128)}, u32[]{:S(2)}) copy-start(s32[2,5,16,2048]{3,2,1,0:T(8,128)} %thr_ref.3) | copy-start | bytes 3932164
  19.2 2.4 %copy-start.2 = (f32[2048]{0:T(1024)S(1)}, f32[2048]{0:T(1024)}, u32[]{:S(2)}) copy-start(f32[2048]{0:T(1024)} %param.9) | copy-start | bytes 24580
  19.2 2.4 %copy-start.3 = (f32[2048]{0:T(1024)S(1)}, f32[2048]{0:T(1024)}, u32[]{:S(2)}) copy-start(f32[2048]{0:T(1024)} %param.10) | copy-start | bytes 24580
  19.4 8.4 %copy-start.6 = (s32[5]{0:T(128)S(1)}, s32[5]{0:T(128)}, u32[]{:S(2)}) copy-start(s32[5]{0:T(128)} %partner_ref.1) | copy-start | bytes 64
  19.4 8.4 %copy-start.7 = (s32[5]{0:T(128)S(1)}, s32[5]{0:T(128)}, u32[]{:S(2)}) copy-start(s32[5]{0:T(128)} %accept_ref.1) | copy-start | bytes 64
  19.4 6.4 %collective-permute-start.5 = (f32[424,128]{1,0:T(8,128)S(1)}, f32[424,128]{1,0:T(8,128)S(1)}, u32[]{:S(2)}, u32[]{:S(2)}) collective-permute-start(f32[424,128]{1,0:T(8,128)S(1)} %get-tuple-element.28), channel_id=1, source_target_pairs={{0,2},{2,4},{4,6},{6,0},{1,3},{3,5},{5,7},{7,1},{8,10},{10,12},{12... | collective-permute-start | bytes 651272 | tf_op jit(solution)/shard_map/ppermute | solution.py:588
  20.0 7.8 %collective-permute-start.6 = (f32[424,128]{1,0:T(8,128)S(1)}, f32[424,128]{1,0:T(8,128)S(1)}, u32[]{:S(2)}, u32[]{:S(2)}) collective-permute-start(f32[424,128]{1,0:T(8,128)S(1)} %get-tuple-element.29), channel_id=1, source_target_pairs={{2,0},{4,2},{6,4},{0,6},{3,1},{5,3},{7,5},{1,7},{10,8},{12,10},{14... | collective-permute-start | bytes 651272 | tf_op jit(solution)/shard_map/ppermute | solution.py:589
  30.7 5.9 %collective-permute-start.7 = (f32[8,128]{1,0:T(8,128)S(1)}, f32[8,128]{1,0:T(8,128)S(1)}, u32[]{:S(2)}, u32[]{:S(2)}) collective-permute-start(f32[8,128]{1,0:T(8,128)S(1)} %get-tuple-element.31), channel_id=1, source_target_pairs={{0,1},{1,0},{2,3},{3,2},{4,5},{5,4},{6,7},{7,6},{8,9},{9,8},{10,11... | collective-permute-start | bytes 12296 | tf_op jit(solution)/shard_map/ppermute | solution.py:614
